TPU v7x, 32 devices: a whole 2x2x4 slice. The times are simulated.
32 devices in a mesh: seq: 8 (over y, x, core), section: 4 (over z).
Axes of the slice: x: 2, y: 2, z: 4, core: 2. Of those that a mesh axis runs over, the one named last changes fastest.
Arguments:
- tokens: bfloat16 [4096, 1024], P('seq'), may hold values from -6 to 6
- input_gain: float32 [4, 1024], P('section'), may hold values from 0.5 to 2
- main_weight: bfloat16 [4, 1024, 4096], P('section'), may hold values from -0.1875 to 0.1875
- side_weight: bfloat16 [4, 1024, 288], P('section'), may hold values from -0.1875 to 0.1875
- conv_kernel: float32 [4, 4, 2304], P('section'), may hold values from -3 to 3
- step_bias: float32 [4, 32], P('section'), may hold values from -4 to 1
- decay_rate: float32 [4, 32], P('section'), may hold values from 0.0001 to 0.04, as said below
- skip_gain: float32 [4, 32], P('section'), may hold values from 1 to 4
- output_gain: float32 [4, 2048], P('section'), may hold values from 0.5 to 2
- output_weight: bfloat16 [4, 2048, 1024], P('section', 'seq'), may hold values from -0.09375 to 0.09375
Outputs:
- layer_outputs: bfloat16 [4, 4096, 1024], P('section', 'seq')
Inputs may be any that keep to these rules, and one draw needn't show every extreme that they name: `decay_rate`: positive.
All inputs are finite; a program needn't handle non-finite values.
Results may differ from a plain program's by a relative error of at most 0.0074.
Values may be sent and summed in bfloat16 or wider, within the bound.
No kernel may reach another device: no remote copies, remote signals or barrier semaphores. Data moves between devices by JAX's collectives and lax.ppermute only.
A program may use at most 128 MiB of HBM per device.

v0:
```python
import functools

import jax
import jax.numpy as jnp
import numpy as np
from jax import lax
from jax.experimental import pallas as pl
from jax.experimental.pallas import tpu as pltpu
from jax.sharding import PartitionSpec as P

EPSILON = 1e-05
CHUNK = 128
WIDTH = (512, 2048)
HALO = 16
EDGE = 32
LIMIT = 28 * 2**20
SMALL = 8 * 2**20
SKEW = 2
REVERSE, UPPER, FIRST, SEQ, RANKS = 0, 1, 2, 3, 4
LOG2E = 1.4426950408889634
F32 = jnp.float32
BF16 = jnp.bfloat16


def silu(value):
    half = 0.5 * value
    return half + half * jnp.tanh(half)


def dot(left, right):
    return jnp.dot(left, right, preferred_element_type=F32)


def time_of(index):
    row = index & (CHUNK - 1)
    return (index - row) + ((row & 7) << 4) + (row >> 3)


def order_matrix(size, reverse, back=False):
    place = lax.broadcasted_iota(jnp.int32, (size, size), 1 if back else 0)
    token = lax.broadcasted_iota(jnp.int32, (size, size), 0 if back else 1)
    time = time_of(place)
    target = jnp.where(reverse == 1, size - 1 - time, time)
    return jnp.where(token == target, 1.0, 0.0).astype(BF16)


def edge_matrix(margin, reverse):
    row = lax.broadcasted_iota(jnp.int32, (EDGE, HALO), 0)
    column = lax.broadcasted_iota(jnp.int32, (EDGE, HALO), 1)
    step = (row >> 3) - (EDGE // 8 - margin)
    source = jnp.where(reverse == 1, margin - 1 - step, HALO - margin + step)
    wanted = (step >= 0) & ((row & 7) == 7) & (column == source)
    return jnp.where(wanted, 1.0, 0.0).astype(BF16)


def high_low(value):
    high = value.astype(BF16)
    low = (value - high.astype(F32)).astype(BF16)
    return jnp.concatenate([high, low], axis=1)


def norm_block(values, gain_row):
    widened = values.astype(F32)
    inverse_rms = lax.rsqrt(jnp.mean(widened * widened, axis=-1, keepdims=True) + EPSILON)
    return (widened * inverse_rms * gain_row).astype(BF16)


def prep_kernel(
    info,
    rows,
    halo,
    gain,
    wide,
    side_weight,
    taps,
    side_taps,
    bias,
    decay,
    spread,
    normed_out,
    x_out,
    b_out,
    c_out,
    cum_out,
    shifted_out,
    reach_out,
    local_out,
    state_out,
    extended,
    buffer,
    turned,
    shares,
    wide_shares,
    running,
):
    step_index = pl.program_id(0)
    reverse = info[REVERSE]
    length = rows.shape[0]
    heads = bias.shape[1]
    state = b_out.shape[1]
    chunks = length // CHUNK
    margin = taps.shape[0] - 1
    width = wide.shape[1]

    def filtered(kernel, c, lanes):
        start = EDGE + c * CHUNK
        tail = 8 * margin
        ending = buffer[start + CHUNK - tail : start + CHUNK, lanes]
        previous = buffer[start - tail : start, lanes]
        leading = lax.broadcasted_iota(jnp.int32, ending.shape, 0) & 7 == 0
        entry = jnp.where(
            leading, pltpu.roll(previous, tail - 7, axis=0), pltpu.roll(ending, 1, axis=0)
        )
        region = jnp.concatenate([entry, buffer[start : start + CHUNK, lanes]], axis=0)
        total = None
        for k in range(margin + 1):
            term = kernel[k : k + 1, lanes] * region[8 * k : 8 * k + CHUNK]
            total = term if total is None else total + term
        return silu(total).astype(BF16)

    @pl.when(step_index == 0)
    def _():
        turn = order_matrix(2 * CHUNK, reverse)
        edge = norm_block(halo[...], gain[...])
        extended[0:EDGE] = dot(edge_matrix(margin, reverse), edge).astype(BF16)
        pairs = length // (2 * CHUNK)
        for pair in range(pairs):
            source = jnp.where(reverse == 1, pairs - 1 - pair, pair) * (2 * CHUNK)
            source = pl.multiple_of(source, 2 * CHUNK)
            piece = norm_block(rows[pl.ds(source, 2 * CHUNK), :], gain[...])
            start = EDGE + pair * 2 * CHUNK
            extended[start : start + 2 * CHUNK] = dot(turn, piece).astype(BF16)
        normed_out[...] = extended[EDGE:]
        side = lax.dot_general(
            extended[...], side_weight[...], (((1,), (1,)), ((), ())), preferred_element_type=F32
        )
        side = side.astype(BF16).astype(F32)
        buffer[:, 0 : 2 * state] = side[:, 0 : 2 * state]
        raw = side[EDGE:, 2 * state :] + bias[...]
        step = jnp.maximum(raw, 0.0) + jnp.log1p(jnp.exp(-jnp.abs(raw)))
        change = step * (decay[...] * (-LOG2E))
        row = lax.broadcasted_iota(jnp.int32, (CHUNK, CHUNK), 0)
        column = lax.broadcasted_iota(jnp.int32, (CHUNK, CHUNK), 1)
        triangle = jnp.where(time_of(row) >= time_of(column), 1.0, 0.0).astype(F32)
        before = jnp.zeros((1, heads), F32)
        totals = []
        befores = []
        for c in range(chunks):
            here = slice(c * CHUNK, (c + 1) * CHUNK)
            cumulative = jnp.dot(
                triangle, change[here], preferred_element_type=F32, precision=lax.Precision.HIGHEST
            )
            last = cumulative[CHUNK - 1 :, :]
            befores.append(before)
            totals.append(last)
            before = before + last
            moved = cumulative - jnp.log2(step[here])
            blank = jnp.zeros((CHUNK, 128 - 2 * heads), F32)
            flipped = jnp.concatenate([cumulative, moved, blank], axis=1).T
            cum_out[:, here] = flipped[0:heads]
            shifted_out[:, here] = flipped[heads : 2 * heads]
            shares[here, :] = high_low(jnp.exp2(last - cumulative) * step[here])
            reach_out[here, :] = high_low(jnp.exp2(cumulative))
        befores.append(before)
        zero_rows = jnp.zeros((HALO - chunks, heads), F32)
        shares[length:, :] = high_low(jnp.exp2(jnp.concatenate(totals + [zero_rows], axis=0)))
        zero_rows = jnp.zeros((HALO - chunks - 1, heads), F32)
        reach_out[length:, :] = high_low(jnp.exp2(jnp.concatenate(befores + [zero_rows], axis=0)))
        for c in range(chunks):
            start = c * CHUNK
            here = slice(start, start + CHUNK)
            in_part = filtered(side_taps, c, slice(0, state))
            b_out[here] = in_part
            flipped = in_part.astype(F32).T.astype(BF16)
            blank = jnp.zeros_like(flipped)
            turned[0:state, here] = flipped if c % 2 == 0 else blank
            turned[state:, here] = blank if c % 2 == 0 else flipped
            c_out[here] = filtered(side_taps, c, slice(state, 2 * state))

    buffer[...] = dot(extended[...], wide[...]).astype(BF16).astype(F32)
    wide_shares[...] = dot(shares[...], spread[...])
    running[...] = jnp.zeros_like(running)
    for pair in range(chunks // 2):
        both = slice(2 * pair * CHUNK, (2 * pair + 2) * CHUNK)
        for lane in range(0, width, 256):
            lanes = slice(lane, lane + 256)
            columns = []
            for inside in (slice(lane, lane + 128), slice(lane + 128, lane + 256)):
                weighted = []
                for c in (2 * pair, 2 * pair + 1):
                    here = slice(c * CHUNK, (c + 1) * CHUNK)
                    piece = filtered(taps, c, inside)
                    x_out[here, inside] = piece
                    weighted.append((piece.astype(F32) * wide_shares[here, inside]).astype(BF16))
                columns.append(jnp.concatenate(weighted, axis=0))
            states = dot(turned[:, both], jnp.concatenate(columns, axis=1))
            entering = running[:, lanes]
            for i, c in enumerate((2 * pair, 2 * pair + 1)):
                local_out[c, :, lanes] = entering.astype(BF16)
                total = wide_shares[length + c : length + c + 1, lanes]
                entering = total * entering + states[i * state : (i + 1) * state]
            running[:, lanes] = entering
    state_out[0:state, :] = running[...].astype(BF16)
    through = wide_shares[length : length + 1, :]
    for c in range(1, chunks):
        through = through * wide_shares[length + c : length + c + 1, :]
    high = through.astype(BF16)
    low = (through - high.astype(F32)).astype(BF16)
    tail = jnp.concatenate(
        [high.astype(F32), low.astype(F32), jnp.zeros((HALO - 2, width), F32)], axis=0
    )
    state_out[state:, :] = tail.astype(BF16)


def mid_kernel(
    normed, gate_weight, x, b, c_rows, cumulative, shifted, skip, spread, y_out, gate_out, scores
):
    step_index = pl.program_id(0)
    length = x.shape[0]
    chunks = length // CHUNK
    heads_here = cumulative.shape[0]
    head_dim = x.shape[1] // heads_here
    row = lax.broadcasted_iota(jnp.int32, (CHUNK, CHUNK), 0)
    column = lax.broadcasted_iota(jnp.int32, (CHUNK, CHUNK), 1)
    causal = time_of(row) >= time_of(column)
    lane = lax.broadcasted_iota(jnp.int32, (CHUNK, 2 * head_dim), 1)

    @pl.when(step_index == 0)
    def _():
        for c in range(chunks):
            here = slice(c * CHUNK, (c + 1) * CHUNK)
            scores[here, :] = lax.dot_general(
                c_rows[here, :], b[here, :], (((1,), (1,)), ((), ())), preferred_element_type=F32
            )

    gate_out[...] = dot(normed[...], gate_weight[...]).astype(BF16)
    skip_rows = jnp.broadcast_to(skip[...], (HALO, skip.shape[1]))
    skips = dot(high_low(skip_rows), spread[...])[0:1]
    for c in range(chunks):
        here = slice(c * CHUNK, (c + 1) * CHUNK)
        score = scores[here, :]
        blank = jnp.zeros((128 - heads_here, CHUNK), F32)
        columns = jnp.concatenate([cumulative[:, here], blank], axis=0).T
        for pair in range(heads_here // 2):
            lanes = slice(2 * pair * head_dim, (2 * pair + 2) * head_dim)
            parts = []
            for h in (2 * pair, 2 * pair + 1):
                gap = columns[:, h : h + 1] - shifted[h : h + 1, here]
                parts.append((score * jnp.exp2(jnp.where(causal, gap, -jnp.inf))).astype(BF16))
            values = x[here, lanes]
            zero = jnp.zeros_like(values)
            stacked = jnp.concatenate(
                [jnp.where(lane < head_dim, values, zero), jnp.where(lane < head_dim, zero, values)],
                axis=0,
            )
            within = dot(jnp.concatenate(parts, axis=1), stacked)
            y_out[here, lanes] = within + skips[:, lanes] * values.astype(F32)


def finish_kernel(plan, shard_rows, members, leading, place_slot, last, info, *refs):
    count = len(members)
    rows, y_all, gate_all, c_all, reach_all, local_all = refs[:6]
    mine, other, partner, gain, spread = refs[6:11]
    rest = refs[11:]
    if plan:
        far_pieces = rest[: len(plan)]
        outs = rest[len(plan) : -4]
        normed, entering, weight, arrived = rest[-4:]
    else:
        weight = rest[0]
        outs = rest[1:-2]
        normed, entering = rest[-2:]
    reverse = info[REVERSE]
    inner = weight.shape[0]
    length = y_all.shape[0]
    state = mine.shape[0]
    block = 256
    fetches = []
    if plan:
        fetches = piece_copies(plan, shard_rows, info, far_pieces, weight, arrived, 0)
    for fetch in fetches:
        fetch.start()
    half = inner // 2
    upper = info[UPPER] == 1
    first = info[FIRST] == 1
    for start in range(0, inner, block):
        lanes = slice(start, start + block)
        inside = slice(start % half, start % half + block)
        pair = (other, mine) if start < half else (mine, other)
        full = jnp.where(upper, pair[0][:, inside], pair[1][:, inside])
        tail = partner[state:, lanes].astype(F32)
        through = tail[0:1] + tail[1:2]
        moved = (through * full.astype(F32) + partner[:state, lanes].astype(F32)).astype(BF16)
        entering[:, lanes] = jnp.where(first, full, moved)
    tail = dot(reach_all[length:, :], spread[...])
    index_row = lax.broadcasted_iota(jnp.int32, (HALO, 1), 0)
    turn = order_matrix(CHUNK, reverse, back=True)
    for i, member in enumerate(members):
        position = jnp.where(reverse == 1, length // CHUNK - 1 - member, member)
        here = pl.ds(pl.multiple_of(position * CHUNK, CHUNK), CHUNK)
        c_rows, reach, local = c_all[here, :], reach_all[here, :], local_all.at[position]
        before = jnp.sum(jnp.where(index_row == position, tail, 0.0), axis=0, keepdims=True)
        squares = jnp.zeros((CHUNK, 1), F32)
        gated = []
        for start in range(0, inner, block):
            lanes = slice(start, start + block)
            full = local[:, lanes].astype(F32) + before[:, lanes] * entering[:, lanes].astype(F32)
            carried = dot(c_rows, full.astype(BF16)) * dot(reach, spread[:, lanes])
            part = (y_all[here, lanes] + carried) * silu(gate_all[here, lanes].astype(F32))
            squares = squares + jnp.sum(part * part, axis=-1, keepdims=True)
            gated.append(part)
        inverse_rms = lax.rsqrt(squares * (1.0 / inner) + EPSILON)
        for index, start in enumerate(range(0, inner, block)):
            lanes = slice(start, start + block)
            piece = (gated[index] * inverse_rms * gain[:, lanes]).astype(BF16)
            normed[i * CHUNK : (i + 1) * CHUNK, lanes] = dot(turn, piece).astype(BF16)
    for fetch in fetches:
        fetch.wait()
    place = info[place_slot]

    def columns(j, carry):
        lanes = pl.ds(j * block if leading else pl.multiple_of(j * block, block), block)
        total = dot(normed[...], weight[:, lanes])
        for i in range(count):
            term = total[i * CHUNK : (i + 1) * CHUNK]
            own = rows[members[i] * CHUNK : (members[i] + 1) * CHUNK, lanes]
            base = own.astype(F32) + term
            if last:
                earlier, sent, base_out = outs[i], outs[count + i], outs[2 * count + i]
                sent[:, lanes] = jnp.where(place == 1, earlier[:, lanes], term.astype(BF16))
                base_out[:, lanes] = base
            else:
                outs[i][:, lanes] = jnp.where(place == 0, term, 0.0).astype(BF16)
                outs[count + i][:, lanes] = jnp.where(place == 1, base, 0.0)
        return carry

    if leading:
        for j in range(weight.shape[1] // block):
            columns(j, 0)
    else:
        lax.fori_loop(0, weight.shape[1] // block, columns, 0)


def kept(shape, dtype):
    return pltpu.VMEM(shape, dtype)


def near(*values):
    return tuple(pltpu.with_memory_space_constraint(v, pltpu.VMEM) for v in values)


def near_one(value):
    return near(value)[0]


def far(value):
    return pltpu.with_memory_space_constraint(value, pltpu.HBM)


def whole_block(shape):
    return pl.BlockSpec(shape, lambda *_: (0,) * len(shape))


def prep(info, rows, halo, params, main, inner, state, resident=False):
    place = near_one if resident else far
    width = min(WIDTH[int(resident)], inner)
    main = place(main)
    gain, side, conv, bias, decay, spread = [place(v) for v in params[:6]]
    length, features = rows.shape
    heads = bias.shape[1]
    steps = inner // width
    chunks = length // CHUNK
    margin = conv.shape[1]
    side_width = 2 * state
    grid_spec = pltpu.PrefetchScalarGridSpec(
        num_scalar_prefetch=1,
        grid=(steps,),
        in_specs=[
            whole_block((length, features)),
            whole_block((HALO, features)),
            whole_block((1, features)),
            pl.BlockSpec((None, features, width), lambda j, _: (0, 0, steps + j)),
            pl.BlockSpec((None, side.shape[1], features), lambda j, _: (0, 0, 0)),
            pl.BlockSpec((None, margin, width), lambda j, _: (0, 0, j)),
            pl.BlockSpec((None, margin, side_width), lambda j, _: (0, 0, inner // side_width)),
            whole_block((1, heads)),
            whole_block((1, heads)),
            pl.BlockSpec((2 * heads, width), lambda j, _: (0, j)),
        ],
        out_specs=[
            whole_block((length, features)),
            pl.BlockSpec((length, width), lambda j, _: (0, j)),
            whole_block((length, state)),
            whole_block((length, state)),
            whole_block((heads, length)),
            whole_block((heads, length)),
            whole_block((length + HALO, 2 * heads)),
            pl.BlockSpec((chunks, state, width), lambda j, _: (0, 0, j)),
            pl.BlockSpec((state + HALO, width), lambda j, _: (0, j)),
        ],
        scratch_shapes=[
            pltpu.VMEM((length + EDGE, features), BF16),
            pltpu.VMEM((length + EDGE, width), F32),
            pltpu.VMEM((2 * state, length), BF16),
            pltpu.VMEM((length + HALO, 2 * heads), BF16),
            pltpu.VMEM((length + HALO, width), F32),
            pltpu.VMEM((state, width), F32),
        ],
    )
    shape = jax.ShapeDtypeStruct
    return pl.pallas_call(
        prep_kernel,
        grid_spec=grid_spec,
        out_shape=[
            kept((length, features), BF16),
            kept((length, inner), BF16),
            kept((length, state), BF16),
            kept((length, state), BF16),
            kept((heads, length), F32),
            kept((heads, length), F32),
            kept((length + HALO, 2 * heads), BF16),
            kept((chunks, state, inner), BF16),
            shape((state + HALO, inner), BF16),
        ],
        compiler_params=pltpu.CompilerParams(
            vmem_limit_bytes=LIMIT, dimension_semantics=("arbitrary",)
        ),
        cost_estimate=pl.CostEstimate(
            flops=2 * length * features * inner, bytes_accessed=12 * 2**20, transcendentals=0
        ),
        name="prep",
    )(info, far(rows), halo, gain, main, side, conv, conv, bias, decay, spread)


def mid(normed, main, x, b, c_rows, cumulative, shifted, params, inner, resident=False):
    place = near_one if resident else far
    width = min(WIDTH[0], inner)
    main, spread, skip = place(main), place(params[5]), place(params[6])
    length, features = normed.shape
    state = b.shape[1]
    steps = inner // width
    heads_here = cumulative.shape[0] // steps
    return pl.pallas_call(
        mid_kernel,
        grid=(steps,),
        in_specs=[
            whole_block((length, features)),
            pl.BlockSpec((None, features, width), lambda j: (0, 0, j)),
            pl.BlockSpec((length, width), lambda j: (0, j)),
            whole_block((length, state)),
            whole_block((length, state)),
            pl.BlockSpec((heads_here, length), lambda j: (j, 0)),
            pl.BlockSpec((heads_here, length), lambda j: (j, 0)),
            whole_block(skip.shape),
            pl.BlockSpec((spread.shape[0], width), lambda j: (0, j)),
        ],
        out_specs=[
            pl.BlockSpec((length, width), lambda j: (0, j)),
            pl.BlockSpec((length, width), lambda j: (0, j)),
        ],
        out_shape=[
            kept((length, inner), F32),
            kept((length, inner), BF16),
        ],
        scratch_shapes=[pltpu.VMEM((length, CHUNK), F32)],
        compiler_params=pltpu.CompilerParams(
            vmem_limit_bytes=LIMIT, dimension_semantics=("arbitrary",)
        ),
        cost_estimate=pl.CostEstimate(
            flops=2 * length * features * inner, bytes_accessed=12 * 2**20, transcendentals=0
        ),
        name="mid",
    )(*near(normed), main, *near(x, b, c_rows, cumulative, shifted), skip, spread)


def finish(
    members, leading, place_slot, last, info, rows, y, gate, c_rows, reach, local, state_parts,
    params, pieces, earlier,
):
    features = rows.shape[1]
    length, inner = y.shape
    state = c_rows.shape[1]
    mine, other, partner = state_parts
    resident = not isinstance(pieces, list)
    place = near_one if resident else far
    spread, gain = place(params[5]), place(params[7])
    plan = [] if resident else [ranges for _, ranges in pieces]
    shard_rows = inner // lax.axis_size("seq")
    count = len(members)
    whole = pl.BlockSpec(memory_space=pltpu.VMEM)
    in_specs = [pl.BlockSpec(memory_space=pltpu.SMEM)]
    in_specs += [whole] * 11
    operands = [rows, *near(y, gate, c_rows, reach, local)]
    in_specs += [whole] if resident else [pl.BlockSpec(memory_space=pl.ANY)] * len(pieces)
    in_specs += [whole] * len(earlier)
    operands += [mine, other, partner, gain, spread]
    operands += [*near(pieces)] if resident else [far(piece) for piece, _ in pieces]
    operands += list(earlier)
    scratch = [pltpu.VMEM((count * CHUNK, inner), BF16), pltpu.VMEM((state, inner), BF16)]
    if not resident:
        scratch.append(pltpu.VMEM((inner, features), BF16))
        scratch.append(pltpu.SemaphoreType.DMA((sum(len(ranges) for ranges in plan),)))
    shape = (CHUNK, features)
    return pl.pallas_call(
        functools.partial(finish_kernel, plan, shard_rows, members, leading, place_slot, last),
        in_specs=in_specs,
        out_specs=[whole] * (2 * count),
        scratch_shapes=scratch,
        out_shape=[jax.ShapeDtypeStruct(shape, BF16)] * count + [kept(shape, F32)] * count,
        compiler_params=pltpu.CompilerParams(
            vmem_limit_bytes=LIMIT
        ),
        cost_estimate=pl.CostEstimate(
            flops=2 * count * CHUNK * features * inner, bytes_accessed=8 * 2**20, transcendentals=0
        ),
        name="finish",
    )(info, *operands)


def hold_kernel(plan, shard_rows, extras, info, *refs):
    main = refs[1]
    far_pieces = refs[2 : 2 + len(plan)]
    small = refs[2 + len(plan) : 2 + len(plan) + extras]
    main_out, weight_out, *small_out, arrived = refs[2 + len(plan) + extras :]
    parts = 4
    rows = main.shape[1] // parts
    copies = []
    for i in range(parts):
        here = pl.ds(i * rows, rows)
        copies.append(
            pltpu.make_async_copy(main.at[0, here], main_out.at[0, here], arrived.at[len(copies)])
        )
    for source, target in zip(small, small_out):
        copies.append(pltpu.make_async_copy(source, target, arrived.at[len(copies)]))
    copies += piece_copies(plan, shard_rows, info, far_pieces, weight_out, arrived, len(copies))
    for copy in copies:
        copy.start()
    for copy in copies:
        copy.wait()


def hold(info, trigger, main, pieces, extras, inner):
    plan = [ranges for _, ranges in pieces]
    features = main.shape[1]
    anywhere = pl.BlockSpec(memory_space=pl.ANY)
    whole = pl.BlockSpec(memory_space=pltpu.VMEM)
    count = 4 + len(extras) + sum(len(ranges) for ranges in plan)
    return pl.pallas_call(
        functools.partial(hold_kernel, plan, inner // lax.axis_size("seq"), len(extras)),
        in_specs=[pl.BlockSpec(memory_space=pltpu.SMEM)]
        + [anywhere] * (2 + len(pieces) + len(extras)),
        out_specs=[whole] * (2 + len(extras)),
        out_shape=[kept(main.shape, BF16), kept((inner, features), BF16)]
        + [kept(v.shape, v.dtype) for v in extras],
        scratch_shapes=[pltpu.SemaphoreType.DMA((count,))],
        compiler_params=pltpu.CompilerParams(vmem_limit_bytes=SMALL),
        cost_estimate=pl.CostEstimate(flops=10**6, bytes_accessed=24 * 2**20, transcendentals=0),
        name="hold",
    )(info, far(trigger), far(main), *[far(piece) for piece, _ in pieces], *[far(v) for v in extras])


def piece_copies(plan, shard_rows, info, far_pieces, weight, arrived, base):
    copies = []
    for piece, ranges in zip(far_pieces, plan):
        for mask, source, offset, extent in ranges:
            place = 0
            if mask is not None:
                place = pl.multiple_of((info[SEQ] ^ mask) * shard_rows + offset, 16)
            copies.append(
                pltpu.make_async_copy(
                    piece.at[source : source + extent],
                    weight.at[pl.ds(place, extent)],
                    arrived.at[base + len(copies)],
                )
            )
    return copies


def stack_kernel(counts, *refs):
    sources, outs = refs[: -len(counts)], refs[-len(counts) :]
    position = 0
    for out, count in zip(outs, counts):
        start = 0
        for source in sources[position : position + count]:
            out[start : start + source.shape[0]] = source[...]
            start += source.shape[0]
        position += count


def stacked(groups):
    operands = []
    specs = []
    out_shape = []
    for group in groups:
        total = 0
        for value, index, rows in group:
            operands.append(value)
            specs.append(pl.BlockSpec((rows, value.shape[1] // 2), lambda j, index=index: (index, j)))
            total += rows
        out_shape.append(pltpu.HBM((total, group[0][0].shape[1]), BF16))
    return pl.pallas_call(
        functools.partial(stack_kernel, [len(group) for group in groups]),
        grid=(2,),
        in_specs=specs,
        out_specs=[
            pl.BlockSpec((shape.shape[0], shape.shape[1] // 2), lambda j: (0, j)) for shape in out_shape
        ],
        out_shape=out_shape,
        compiler_params=pltpu.CompilerParams(vmem_limit_bytes=16 * 2**20),
        cost_estimate=pl.CostEstimate(flops=10**6, bytes_accessed=10**6, transcendentals=0),
        name="stack",
    )(*[far(value) for value in operands])


def seq_swap(value, mask):
    count = lax.axis_size("seq")
    return lax.ppermute(value, "seq", [(i, i ^ mask) for i in range(count)])


def split_state(packed):
    state = packed.shape[0] - HALO
    values = packed[:state].astype(F32)
    tail = packed[state:].astype(F32)
    return values, tail[0:1] + tail[1:2]


def joined_state(values, through):
    high = through.astype(BF16)
    low = (through - high.astype(F32)).astype(BF16)
    rest = jnp.zeros((HALO - 2, through.shape[1]), F32)
    tail = jnp.concatenate([high.astype(F32), low.astype(F32), rest], axis=0)
    return values.astype(BF16), tail.astype(BF16)


def after(earlier, later):
    return later[1] * earlier[0] + later[0], earlier[1] * later[1]


def chosen(condition, first, second):
    return tuple(jnp.where(condition, a, b) for a, b in zip(first, second))


def pair_kernel(info, mine, partner, out):
    half = out.shape[1]
    first = info[FIRST] == 1
    state = out.shape[0] - HALO
    for start in range(0, half, 256):
        place = pl.multiple_of(info[UPPER] * half + start, 256)
        one = split_state(mine[:, pl.ds(place, 256)])
        two = split_state(partner[:, pl.ds(place, 256)])
        total = after(chosen(first, one, two), chosen(first, two, one))
        out[:state, start : start + 256], out[state:, start : start + 256] = joined_state(*total)


def merge_kernel(group, slot, has_entering, last, info, *refs):
    members = refs[: 2**group]
    entering_out = refs[2**group + has_entering]
    rank = info[slot]
    state, half = entering_out.shape
    for start in range(0, half, 256):
        lanes = slice(start, start + 256)
        values = [split_state(member[:, lanes]) for member in members]
        before = (jnp.zeros((state, 256), F32), jnp.ones((1, 256), F32))
        whole = before
        for place in range(2**group):
            value = values[0]
            for code in range(1, 2**group):
                value = chosen((rank ^ code) == place, values[code], value)
            if place < 2**group - 1:
                before = chosen(place < rank, after(before, value), before)
            if not last:
                whole = after(whole, value)
        if has_entering:
            inside = refs[2**group][:, lanes].astype(F32)
            through = jnp.ones((1, 256), F32)
            before = after(before, (inside, through))
        entering_out[:, lanes] = before[0].astype(BF16)
        if not last:
            out = refs[-1]
            out[:state, lanes], out[state:, lanes] = joined_state(*whole)


def small_call(kernel, name, out_shape, info, *operands):
    return pl.pallas_call(
        kernel,
        in_specs=[pl.BlockSpec(memory_space=pltpu.SMEM)] + [whole_block(v.shape) for v in operands],
        out_specs=[whole_block(v.shape) for v in out_shape],
        out_shape=out_shape,
        compiler_params=pltpu.CompilerParams(vmem_limit_bytes=SMALL),
        cost_estimate=pl.CostEstimate(flops=10**6, bytes_accessed=10**6, transcendentals=0),
        name=name,
    )(info, *operands)


def settle_kernel(place, info, base, sent, other, *rest):
    section = info[place]
    rows = (base[...] + other[...].astype(F32)).astype(BF16)
    rows = jnp.where(section == 1, sent[...], rows)
    rest[-1][...] = jnp.where(section == 0, other[...], rows)


def settle(index, chunks, place, info, base, sent, other, finished):
    features = base.shape[1]
    length = chunks * CHUNK
    out_block = pl.BlockSpec((None, CHUNK, features), lambda j: (0, index, 0))
    passed = [] if finished is None else [finished]
    return pl.pallas_call(
        functools.partial(settle_kernel, place),
        grid=(1,),
        in_specs=[pl.BlockSpec(memory_space=pltpu.SMEM)]
        + [whole_block((CHUNK, features))] * 3
        + [pl.BlockSpec(memory_space=pl.ANY)] * len(passed),
        out_specs=out_block,
        out_shape=jax.ShapeDtypeStruct((1, length, features), BF16),
        input_output_aliases={4: 0} if passed else {},
        compiler_params=pltpu.CompilerParams(vmem_limit_bytes=SMALL),
        cost_estimate=pl.CostEstimate(flops=10**6, bytes_accessed=10**6, transcendentals=0),
        name="settle",
    )(info, base, sent, other, *passed)


def stages_of(seq_count):
    bits = seq_count.bit_length() - 1
    found = []
    bit = 1
    while bit < bits:
        group = min(2, bits - bit)
        found.append((bit, group))
        bit += group
    return found


def entering_state(packed, info, sections, seq_count, meanwhile):
    section_count = lax.axis_size("section")
    stages = stages_of(seq_count)

    def swap(value, mask):
        pairs = [
            (i * section_count + s, (i ^ mask) * section_count + s)
            for s in sections
            for i in range(seq_count)
        ]
        return lax.ppermute(value, ("seq", "section"), pairs)

    def forward(value, mask, low_bit):
        pairs = []
        for s in sections:
            for i in range(seq_count):
                later = (i ^ mask) >> low_bit > i >> low_bit
                if later == (s % 2 == 0):
                    pairs.append((i * section_count + s, (i ^ mask) * section_count + s))
        return lax.ppermute(value, ("seq", "section"), pairs)

    depth, inner = packed.shape
    half = jax.ShapeDtypeStruct((depth, inner // 2), BF16)
    states = jax.ShapeDtypeStruct((depth - HALO, inner // 2), BF16)
    partner = swap(packed, 1)
    (total,) = small_call(pair_kernel, "pair", [half], info, packed, partner)
    done = meanwhile(total)
    info, _ = lax.optimization_barrier((info, done[0]))
    entering = []
    for index, (bit, group) in enumerate(stages):
        last = index + 1 == len(stages)
        members = [total]
        for code in range(1, 2**group):
            mask = code << bit
            members.append(forward(total, mask, bit) if last else swap(total, mask))
        kernel = functools.partial(merge_kernel, group, RANKS + index, len(entering), last)
        shapes = [states] if last else [states, half]
        results = small_call(kernel, "merge", shapes, info, *members, *entering)
        entering = [results[0]]
        total = results[-1]
    return (entering[0], swap(entering[0], 1), partner), done


def per_device(
    tokens,
    input_gain,
    main_weight,
    side_weight,
    conv_kernel,
    step_bias,
    decay_rate,
    skip_gain,
    output_gain,
    output_weight,
):
    length, features = tokens.shape
    inner = main_weight.shape[2] // 2
    heads = decay_rate.shape[1]
    state = (side_weight.shape[2] - heads) // 2
    head_dim = inner // heads
    chunks = length // CHUNK
    seq_count = lax.axis_size("seq")
    section_count = lax.axis_size("section")
    section_index = lax.axis_index("section")
    seq_index = lax.axis_index("seq")
    reverse = section_index % 2
    shard = output_weight[0]
    expand = np.repeat(np.eye(heads, dtype=np.float32), head_dim, axis=1)
    spread = jnp.asarray(np.concatenate([expand, expand], axis=0), BF16)
    upper = seq_index % 2
    facts = [reverse, upper, (upper == reverse).astype(jnp.int32), seq_index]
    for bit, group in stages_of(seq_count):
        position = (seq_index >> bit) % 2**group
        facts.append(jnp.where(reverse == 1, 2**group - 1 - position, position))
    places = len(facts)
    rounds = section_count // 2
    for round_index in range(rounds):
        facts.append(section_index - 2 * round_index)
    info = jnp.stack([fact.astype(jnp.int32) for fact in facts])
    order = [chunks - 1, 0] + list(range(1, chunks - 1))

    def edges(first_rows, last_rows, first_wanted, sources, targets):
        pairs = []
        for source, target in zip(sources, targets):
            for i in range(seq_count):
                beside = i + 1 if target % 2 == 0 else i - 1
                if 0 <= beside < seq_count:
                    pairs.append((i * section_count + source, beside * section_count + target))
        value = jnp.where(first_wanted, first_rows, last_rows)
        return lax.ppermute(value, ("seq", "section"), pairs)

    current = tokens
    halo = edges(tokens[:HALO], tokens[length - HALO :], reverse == 1, (0, 1), (0, 1))
    previous = None
    shards = None
    if seq_count == 8:
        halo, shard = lax.optimization_barrier((halo, shard))
        shards = [shard, seq_swap(shard, 2), seq_swap(shard, 4)]
        pieces = None
    else:
        whole = lax.all_gather(shard, "seq", axis=0, tiled=True)
        pieces = [(whole, [(None, 0, 0, inner)])]
    main = main_weight
    params = [
        input_gain, jnp.swapaxes(side_weight, 1, 2), conv_kernel, step_bias, decay_rate, spread,
        skip_gain, output_gain,
    ]
    for round_index in range(rounds):
        active = (2 * round_index, 2 * round_index + 1)
        normed, x, b, c_rows, cumulative, shifted, reach, local, packed = prep(
            info,
            current,
            halo,
            params,
            main,
            inner,
            state,
            round_index > 0,
        )
        early = round_index == 0 and shards
        if early:
            packed, *shards[1:] = lax.optimization_barrier((packed, *shards[1:]))

        def meanwhile(total, normed=normed):
            nonlocal pieces
            if early:
                *parts, _ = lax.optimization_barrier((*shards, total))
                rows = parts[0].shape[0] // 2
                up, down, three = stacked(
                    [
                        [(parts[2], 0, rows)],
                        [(parts[1], 1, rows)],
                        [(part, 0, 2 * rows) for part in parts],
                    ]
                )
                halves = [seq_swap(up, 2), seq_swap(down, 4)]
                swapped = seq_swap(three, 1)
            ready, _ = lax.optimization_barrier((normed, total))
            y, gate = mid(
                ready, main, x, b, c_rows, cumulative, shifted, params, inner,
                round_index > 0,
            )
            if early:
                *halves, _ = lax.optimization_barrier((*halves, y))
                rows = halves[0].shape[0]
                (joined,) = stacked([[(half, 0, rows) for half in halves]])
                diagonal = seq_swap(joined, 1)
                pieces = [(value, [(mask, 0, 0, 2 * rows)]) for value, mask in zip(shards, (0, 2, 4))]
                pieces += [(half, [(6, 0, i * rows, rows)]) for i, half in enumerate(halves)]
                pieces.append((swapped, [(m, i * 2 * rows, 0, 2 * rows) for i, m in enumerate((1, 3, 5))]))
                pieces.append((diagonal, [(7, 0, 0, 2 * rows)]))
            return y, gate

        state_parts, (y, gate) = entering_state(packed, info, active, seq_count, meanwhile)
        last_round = round_index + 1 == rounds
        low, high = active
        place = section_index - low
        terms = {}
        bases = {}
        for members in (order[: chunks // 2], order[chunks // 2 :]):
            outs = finish(
                tuple(members), members[0] == order[0], places if last_round else places + round_index, last_round, info,
                current, y, gate, c_rows, reach, local, state_parts, params, pieces,
                [previous[member] for member in members] if last_round else [],
            )
            for i, member in enumerate(members):
                terms[member] = outs[i]
                bases[member] = outs[len(members) + i]
        if last_round:
            break
        received = []
        values = []
        direct = None
        for step in range(chunks + 2 * SKEW - 1):
            pairs = [(low + hop, low + hop + 1) for hop in range(3) if 0 <= step - hop * SKEW < chunks]
            value = terms[order[step]] if step < chunks else None
            if step >= SKEW:
                passed = received[step - SKEW]
                if step - SKEW < chunks:
                    total = bases[order[step - SKEW]] + passed.astype(F32)
                    total = total if value is None else total + value.astype(F32)
                    passed = total.astype(BF16)
                value = passed
            values.append(value)
            received.append(lax.ppermute(value, "section", pairs))
            if step == chunks + SKEW - 1:
                direct = lax.ppermute(value, "section", [(low + 1, low + 3)])
        received.append(direct)
        trigger, _ = lax.optimization_barrier((values[chunks + SKEW - 1], received[2 * SKEW]))
        main, pieces, *params = hold(info, trigger, main_weight, pieces, params, inner)
        last_rows = jnp.where(place == 3, received[2 * SKEW], received[SKEW])[CHUNK - HALO :]
        first_rows = jnp.where(place == 3, received[2 * SKEW + 1], received[SKEW + 1])[:HALO]
        halo = edges(first_rows, last_rows, reverse == 1, (low + 2, high + 2), (low + 2, high + 2))
        received[-1], received[-2], halo = lax.optimization_barrier((received[-1], received[-2], halo))
        layer_rows = [None] * chunks
        next_rows = [None] * chunks
        for step, index in enumerate(order):
            layer_rows[index] = values[step + SKEW]
            next_rows[index] = jnp.where(place == 3, received[step + 2 * SKEW], received[step + SKEW])
        previous = layer_rows
        current = jnp.concatenate(next_rows, axis=0)
    finished = None
    for index in order:
        other = lax.ppermute(terms[index], "section", [(low, high), (high, low), (1, 0)])
        finished = settle(index, chunks, places, info, bases[index], terms[index], other, finished)
    return finished


def solution(mesh):
    placed = (
        P("seq", None),
        P("section", None),
        P("section", None, None),
        P("section", None, None),
        P("section", None, None),
        P("section", None),
        P("section", None),
        P("section", None),
        P("section", None),
        P("section", "seq", None),
    )
    return jax.shard_map(
        per_device, mesh=mesh, in_specs=placed, out_specs=P("section", "seq", None), check_vma=False
    )
```

profile of v0, /device:TPU:20, one launch (start us, length us, event | category | flops | bytes accessed | tf_op | source)
XLA Modules:
  0.0 174.9 jit_solution(738009553125811925)
XLA Ops:
  2.0 1.5 collective-permute-start.1
  3.6 10.9 %prep.2 = (bf16[512,1024]{1,0:T(8,128)(2,1)S(1)}, bf16[512,2048]{1,0:T(8,128)(2,1)S(1)}, bf16[512,128]{1,0:T(8,128)(2,1)S(1)}, bf16[512,128]{1,0:T(8,128)(2,1)S(...) custom-call(s32[7]{0:T(128)S(1)} %stack.37.info, ...), custom_call_target="tpu_custom_call" | custom-call | flops 2147483648 | bytes 12582912 | tf_op jit(solution)/shard_map/prep/pallas_call | solution.py:411
  17.0 2.7 %stack.39 = (bf16[128,1024]{1,0:T(8,128)(2,1)}, bf16[128,1024]{1,0:T(8,128)(2,1)}, bf16[768,1024]{1,0:T(8,128)(2,1)}) custom-call(bf16[256,1024]{1,0:T(8,128)(2,1)} %copy-done.5, bf16[256,1024]{1,0:T(8,128)(2,1)} %copy-done.6, bf16[256,1024]{1,0:T(8,128)(2,1)} %bitcast.11, bf16[256,1024]{1,0:T(8,128)(2,1)} %copy-done.6, bf16[256,1024]{1,0:T(8,128)(2,1)} %copy-done.5), custom_call_target="tpu_custom_call" | custom-call | flops 1000000 | bytes 1000000 | tf_op jit(solution)/shard_map/stack/pallas_call | solution.py:601
  19.8 1.6 collective-permute-start.8
  21.3 1.5 collective-permute-start.9
  24.2 4.5 %collective-permute-done.8.refs_0_.refs_14_.refs_5_ = bf16[128,1024]{1,0:T(8,128)(2,1)S(1)} collective-permute-done((bf16[128,1024]{1,0:T(8,128)(2,1)}, bf16[128,1024]{1,0:T(8,128)(2,1)S(1)}, u32[]{:S(2)}, u32[]{:S(2)}) %collective-permute-start.8) | collective-permute-done | bytes 262176 | tf_op jit(solution)/shard_map/ppermute | solution.py:617
  29.4 6.8 %mid.2 = (f32[512,2048]{1,0:T(8,128)S(1)}, bf16[512,2048]{1,0:T(8,128)(2,1)S(1)}) custom-call(bf16[512,1024]{1,0:T(8,128)(2,1)S(1)} %get-tuple-element.79.normed, bf16[1,1024,4096]{2,1,0:T(8,128)(2,1)} %refs_1_.1, bf16[512,2048]{1,0:T(8,128)(2,1)S(1)} %get-tuple-element.80.x, bf16[512,128]{1,0:T(8,128)(2,1)S(1)} %get-tuple-element.81.b, ...), custom_call_target="tpu_custom_call" | custom-call | flops 2147483648 | bytes 12582912 | tf_op jit(solution)/shard_map/mid/pallas_call | solution.py:443
  36.9 1.8 %stack.40 = bf16[256,1024]{1,0:T(8,128)(2,1)} custom-call(bf16[128,1024]{1,0:T(8,128)(2,1)} %copy-done.8, bf16[128,1024]{1,0:T(8,128)(2,1)} %copy-done.9), custom_call_target="tpu_custom_call" | custom-call | flops 1000000 | bytes 1000000 | tf_op jit(solution)/shard_map/stack/pallas_call | solution.py:601
  38.8 0.9 merge.2.refs_6_
  42.2 6.0 %finish.5 = (bf16[128,1024]{1,0:T(8,128)(2,1)S(1)}, bf16[128,1024]{1,0:T(8,128)(2,1)S(1)}, f32[128,1024]{1,0:T(8,128)S(1)}, f32[128,1024]{1,0:T(8,128)S(1)}) custom-call(s32[7]{0:T(128)S(1)} %stack.37.info, bf16[512,1024]{1,0:T(8,128)(2,1)S(1)} %copy-done.1, f32[512,2048]{1,0:T(8,128)S(1)} %get-tuple-element.85.refs_1_, ...), custom_call_target="tpu_custom_call" | custom-call | flops 1073741824 | bytes 8388608 | tf_op jit(solution)/shard_map/finish/pallas_call | solution.py:504
  48.9 0.9 collective-permute-start.12
  49.8 6.6 %finish.4 = (bf16[128,1024]{1,0:T(8,128)(2,1)S(1)}, bf16[128,1024]{1,0:T(8,128)(2,1)S(1)}, f32[128,1024]{1,0:T(8,128)S(1)}, f32[128,1024]{1,0:T(8,128)S(1)}) custom-call(s32[7]{0:T(128)S(1)} %stack.37.info, bf16[512,1024]{1,0:T(8,128)(2,1)S(1)} %copy-done.1, f32[512,2048]{1,0:T(8,128)S(1)} %get-tuple-element.85.refs_1_, ...), custom_call_target="tpu_custom_call" | custom-call | flops 1073741824 | bytes 8388608 | tf_op jit(solution)/shard_map/finish/pallas_call | solution.py:504
  56.5 1.3 collective-permute-start.17
  57.9 1.3 collective-permute-start.13
  59.2 19.9 %collective-permute-done.17 = bf16[128,1024]{1,0:T(8,128)(2,1)S(1)} collective-permute-done((bf16[128,1024]{1,0:T(8,128)(2,1)S(1)}, bf16[128,1024]{1,0:T(8,128)(2,1)S(1)}, u32[]{:S(2)}, u32[]{:S(2)}) %collective-permute-start.17) | collective-permute-done | bytes 262176 | tf_op jit(solution)/shard_map/ppermute | solution.py:917
  79.2 1.9 %collective-permute-start.18 = (bf16[128,1024]{1,0:T(8,128)(2,1)S(1)}, bf16[128,1024]{1,0:T(8,128)(2,1)S(1)}, u32[]{:S(2)}, u32[]{:S(2)}) collective-permute-start(bf16[128,1024]{1,0:T(8,128)(2,1)S(1)} %add_convert_fusion.refs_12_), channel_id=1, source_target_pairs={{1,2},{2,3},{5,6},{6,7},{9,10},{10,11},{13,14},{14,15},{17,18},{18... | collective-permute-start | bytes 786440 | tf_op jit(solution)/shard_map/ppermute | solution.py:917
  81.1 4.2 %collective-permute-done.13 = bf16[128,1024]{1,0:T(8,128)(2,1)S(1)} collective-permute-done((bf16[128,1024]{1,0:T(8,128)(2,1)S(1)}, bf16[128,1024]{1,0:T(8,128)(2,1)S(1)}, u32[]{:S(2)}, u32[]{:S(2)}) %collective-permute-start.13) | collective-permute-done | bytes 262176 | tf_op jit(solution)/shard_map/ppermute | solution.py:917
  85.4 1.9 %collective-permute-start.14 = (bf16[128,1024]{1,0:T(8,128)(2,1)S(1)}, bf16[128,1024]{1,0:T(8,128)(2,1)S(1)}, u32[]{:S(2)}, u32[]{:S(2)}) collective-permute-start(bf16[128,1024]{1,0:T(8,128)(2,1)S(1)} %add_convert_fusion.2.refs_0_.refs_13_), channel_id=1, source_target_pairs={{1,2},{2,3},{5,6},{6,7},{9,10},{10,11},{13,14},{14,15},{17,18},{18... | collective-permute-start | bytes 786440 | tf_op jit(solution)/shard_map/ppermute | solution.py:917
  88.1 2.9 %collective-permute-done.18 = bf16[128,1024]{1,0:T(8,128)(2,1)S(1)} collective-permute-done((bf16[128,1024]{1,0:T(8,128)(2,1)S(1)}, bf16[128,1024]{1,0:T(8,128)(2,1)S(1)}, u32[]{:S(2)}, u32[]{:S(2)}) %collective-permute-start.18) | collective-permute-done | bytes 262176 | tf_op jit(solution)/shard_map/ppermute | solution.py:917
  91.0 1.3 collective-permute-start.19
  92.3 4.5 %collective-permute-done.14 = bf16[128,1024]{1,0:T(8,128)(2,1)S(1)} collective-permute-done((bf16[128,1024]{1,0:T(8,128)(2,1)S(1)}, bf16[128,1024]{1,0:T(8,128)(2,1)S(1)}, u32[]{:S(2)}, u32[]{:S(2)}) %collective-permute-start.14) | collective-permute-done | bytes 262176 | tf_op jit(solution)/shard_map/ppermute | solution.py:917
  96.8 1.9 %collective-permute-start.20 = (bf16[16,1024]{1,0:T(8,128)(2,1)S(1)}, bf16[16,1024]{1,0:T(8,128)(2,1)S(1)}, u32[]{:S(2)}, u32[]{:S(2)}) collective-permute-start(bf16[16,1024]{1,0:T(8,128)(2,1)S(1)} %slice_select_fusion), channel_id=1, source_target_pairs={{2,6},{6,10},{10,14},{14,18},{18,22},{22,26},{26,30},{7,3},{11,7},... | collective-permute-start | bytes 98312 | tf_op jit(solution)/shard_map/ppermute | solution.py:822
  98.7 5.6 %hold.1 = (bf16[1,1024,4096]{2,1,0:T(8,128)(2,1)S(1)}, bf16[2048,1024]{1,0:T(8,128)(2,1)S(1)}, f32[1,1024]{1,0:T(1,128)S(1)}, bf16[1,288,1024]{2,1,0:T(8,128)(2,...) custom-call(s32[7]{0:T(128)S(1)} %stack.37.info, ...), custom_call_target="tpu_custom_call" | custom-call | flops 1000000 | bytes 25165824 | tf_op jit(solution)/shard_map/hold/pallas_call | solution.py:548
  104.5 1.0 pad_maximum_fusion.rows.refs_0_
  105.5 8.6 %prep.3 = (bf16[512,1024]{1,0:T(8,128)(2,1)S(1)}, bf16[512,2048]{1,0:T(8,128)(2,1)S(1)}, bf16[512,128]{1,0:T(8,128)(2,1)S(1)}, bf16[512,128]{1,0:T(8,128)(2,1)S(...) custom-call(s32[7]{0:T(128)S(1)} %stack.37.info, ...), custom_call_target="tpu_custom_call" | custom-call | flops 2147483648 | bytes 12582912 | tf_op jit(solution)/shard_map/prep/pallas_call | solution.py:411
  114.1 3.6 %collective-permute-start.21 = (bf16[144,2048]{1,0:T(8,128)(2,1)S(1)}, bf16[144,2048]{1,0:T(8,128)(2,1)S(1)}, u32[]{:S(2)}, u32[]{:S(2)}) collective-permute-start(bf16[144,2048]{1,0:T(8,128)(2,1)S(1)} %get-tuple-element.120.mine), channel_id=1, source_target_pairs={{2,6},{6,2},{10,14},{14,10},{18,22},{22,18},{26,30},{30,26},{3,7},... | collective-permute-start | bytes 1769480 | tf_op jit(solution)/shard_map/ppermute | solution.py:743
  117.7 1.6 collective-permute-done.21.partner.refs_8_
  120.0 1.3 collective-permute-start.24
  121.3 1.3 collective-permute-start.23
  122.6 2.4 %collective-permute-start.22 = (bf16[144,1024]{1,0:T(8,128)(2,1)S(1)}, bf16[144,1024]{1,0:T(8,128)(2,1)S(1)}, u32[]{:S(2)}, u32[]{:S(2)}) collective-permute-start(bf16[144,1024]{1,0:T(8,128)(2,1)S(1)} %pair.3.refs_0_), channel_id=1, source_target_pairs={{2,10},{6,14},{18,26},{22,30},{11,3},{15,7},{27,19},{31,23}} | collective-permute-start | bytes 884744 | tf_op jit(solution)/shard_map/ppermute | solution.py:752
  125.0 5.9 %mid.3 = (f32[512,2048]{1,0:T(8,128)S(1)}, bf16[512,2048]{1,0:T(8,128)(2,1)S(1)}) custom-call(bf16[512,1024]{1,0:T(8,128)(2,1)S(1)} %get-tuple-element.121.normed, bf16[1,1024,4096]{2,1,0:T(8,128)(2,1)S(1)} %get-tuple-element.113.wide.gate_weight, bf16[512,2048]{1,0:T(8,128)(2,1)S(1)} %get-tuple-element.122.x, bf16[512,128]{1,0:T(8,128)(2,1)S(1)} %get-tuple-element.123.b, ...), custom_call_target="tpu_custom_call" | custom-call | flops 2147483648 | bytes 12582912 | tf_op jit(solution)/shard_map/mid/pallas_call | solution.py:443
  131.0 1.2 collective-permute-done.24.refs_3_
  132.2 6.2 %collective-permute-done.23.refs_2_ = bf16[144,1024]{1,0:T(8,128)(2,1)S(1)} collective-permute-done((bf16[144,1024]{1,0:T(8,128)(2,1)S(1)}, bf16[144,1024]{1,0:T(8,128)(2,1)S(1)}, u32[]{:S(2)}, u32[]{:S(2)}) %collective-permute-start.23) | collective-permute-done | bytes 294944 | tf_op jit(solution)/shard_map/ppermute | solution.py:752
  138.4 0.9 merge.3.refs_6_
  139.4 2.0 %collective-permute-start.25 = (bf16[128,1024]{1,0:T(8,128)(2,1)S(1)}, bf16[128,1024]{1,0:T(8,128)(2,1)S(1)}, u32[]{:S(2)}, u32[]{:S(2)}) collective-permute-start(bf16[128,1024]{1,0:T(8,128)(2,1)S(1)} %merge.3.refs_6_), channel_id=1, source_target_pairs={{2,6},{6,2},{10,14},{14,10},{18,22},{22,18},{26,30},{30,26},{3,7},... | collective-permute-start | bytes 786440 | tf_op jit(solution)/shard_map/ppermute | solution.py:743
  141.3 1.5 collective-permute-done.25.refs_7_
  142.8 3.7 %finish.7 = (bf16[128,1024]{1,0:T(8,128)(2,1)S(1)}, bf16[128,1024]{1,0:T(8,128)(2,1)S(1)}, f32[128,1024]{1,0:T(8,128)S(1)}, f32[128,1024]{1,0:T(8,128)S(1)}) custom-call(s32[7]{0:T(128)S(1)} %stack.37.info, bf16[512,1024]{1,0:T(8,128)(2,1)S(1)} %copy-done, f32[512,2048]{1,0:T(8,128)S(1)} %get-tuple-element.128.refs_1_, ...), custom_call_target="tpu_custom_call" | custom-call | flops 1073741824 | bytes 8388608 | tf_op jit(solution)/shard_map/finish/pallas_call | solution.py:504
  146.5 2.0 %collective-permute-start.28 = (bf16[128,1024]{1,0:T(8,128)(2,1)S(1)}, bf16[128,1024]{1,0:T(8,128)(2,1)S(1)}, u32[]{:S(2)}, u32[]{:S(2)}) collective-permute-start(bf16[128,1024]{1,0:T(8,128)(2,1)S(1)} %get-tuple-element.140.sent), channel_id=1, source_target_pairs={{2,3},{3,2},{1,0},{6,7},{7,6},{5,4},{10,11},{11,10},{9,8},{14,15},... | collective-permute-start | bytes 786440 | tf_op jit(solution)/shard_map/ppermute | solution.py:936
  148.5 3.9 %collective-permute-start.29 = (bf16[128,1024]{1,0:T(8,128)(2,1)S(1)}, bf16[128,1024]{1,0:T(8,128)(2,1)S(1)}, u32[]{:S(2)}, u32[]{:S(2)}) collective-permute-start(bf16[128,1024]{1,0:T(8,128)(2,1)S(1)} %get-tuple-element.142.sent), channel_id=1, source_target_pairs={{2,3},{3,2},{1,0},{6,7},{7,6},{5,4},{10,11},{11,10},{9,8},{14,15},... | collective-permute-start | bytes 786440 | tf_op jit(solution)/shard_map/ppermute | solution.py:936
  152.4 4.4 %finish.6 = (bf16[128,1024]{1,0:T(8,128)(2,1)S(1)}, bf16[128,1024]{1,0:T(8,128)(2,1)S(1)}, f32[128,1024]{1,0:T(8,128)S(1)}, f32[128,1024]{1,0:T(8,128)S(1)}) custom-call(s32[7]{0:T(128)S(1)} %stack.37.info, bf16[512,1024]{1,0:T(8,128)(2,1)S(1)} %copy-done, f32[512,2048]{1,0:T(8,128)S(1)} %get-tuple-element.128.refs_1_, ...), custom_call_target="tpu_custom_call" | custom-call | flops 1073741824 | bytes 8388608 | tf_op jit(solution)/shard_map/finish/pallas_call | solution.py:504
  156.8 2.0 %collective-permute-start.27 = (bf16[128,1024]{1,0:T(8,128)(2,1)S(1)}, bf16[128,1024]{1,0:T(8,128)(2,1)S(1)}, u32[]{:S(2)}, u32[]{:S(2)}) collective-permute-start(bf16[128,1024]{1,0:T(8,128)(2,1)S(1)} %get-tuple-element.138.sent), channel_id=1, source_target_pairs={{2,3},{3,2},{1,0},{6,7},{7,6},{5,4},{10,11},{11,10},{9,8},{14,15},... | collective-permute-start | bytes 786440 | tf_op jit(solution)/shard_map/ppermute | solution.py:936
  158.8 3.9 %collective-permute-start.26 = (bf16[128,1024]{1,0:T(8,128)(2,1)S(1)}, bf16[128,1024]{1,0:T(8,128)(2,1)S(1)}, u32[]{:S(2)}, u32[]{:S(2)}) collective-permute-start(bf16[128,1024]{1,0:T(8,128)(2,1)S(1)} %get-tuple-element.136.sent), channel_id=1, source_target_pairs={{2,3},{3,2},{1,0},{6,7},{7,6},{5,4},{10,11},{11,10},{9,8},{14,15},... | collective-permute-start | bytes 786440 | tf_op jit(solution)/shard_map/ppermute | solution.py:936
  163.2 1.3 settle.4.rest_0_
  164.5 1.3 settle.5.rest_0_
  165.8 3.0 %collective-permute-done.27.other = bf16[128,1024]{1,0:T(8,128)(2,1)S(1)} collective-permute-done((bf16[128,1024]{1,0:T(8,128)(2,1)S(1)}, bf16[128,1024]{1,0:T(8,128)(2,1)S(1)}, u32[]{:S(2)}, u32[]{:S(2)}) %collective-permute-start.27) | collective-permute-done | bytes 262176 | tf_op jit(solution)/shard_map/ppermute | solution.py:936
  168.8 1.3 settle.6.rest_0_
  170.1 3.5 %collective-permute-done.26.other = bf16[128,1024]{1,0:T(8,128)(2,1)S(1)} collective-permute-done((bf16[128,1024]{1,0:T(8,128)(2,1)S(1)}, bf16[128,1024]{1,0:T(8,128)(2,1)S(1)}, u32[]{:S(2)}, u32[]{:S(2)}) %collective-permute-start.26) | collective-permute-done | bytes 262176 | tf_op jit(solution)/shard_map/ppermute | solution.py:936
  173.6 1.3 settle.7
  (62 shorter events, 12.7 us)
Async XLA Ops:
  0.8 0.7 collective-permute-start
  1.5 13.9 %collective-permute-start.2 = (bf16[256,1024]{1,0:T(8,128)(2,1)}, bf16[256,1024]{1,0:T(8,128)(2,1)S(1)}, u32[]{:S(2)}, u32[]{:S(2)}) collective-permute-start(bf16[256,1024]{1,0:T(8,128)(2,1)} %bitcast.9), channel_id=1, source_target_pairs={{0,16},{4,20},{8,24},{12,28},{16,0},{20,4},{24,8},{28,12},{1,17},{... | collective-permute-start | bytes 1572872 | tf_op jit(solution)/shard_map/ppermute | solution.py:617
  2.0 13.6 %collective-permute-start.1 = (bf16[256,1024]{1,0:T(8,128)(2,1)}, bf16[256,1024]{1,0:T(8,128)(2,1)S(1)}, u32[]{:S(2)}, u32[]{:S(2)}) collective-permute-start(bf16[256,1024]{1,0:T(8,128)(2,1)} %bitcast.10), channel_id=1, source_target_pairs={{0,8},{4,12},{8,0},{12,4},{16,24},{20,28},{24,16},{28,20},{1,9},{5... | collective-permute-start | bytes 1572872 | tf_op jit(solution)/shard_map/ppermute | solution.py:617
  15.4 1.6 copy-start.5
  15.6 1.4 copy-start.6
  15.6 0.7 collective-permute-start.3
  19.8 21.1 %collective-permute-start.10 = (bf16[768,1024]{1,0:T(8,128)(2,1)}, bf16[768,1024]{1,0:T(8,128)(2,1)S(1)}, u32[]{:S(2)}, u32[]{:S(2)}) collective-permute-start(bf16[768,1024]{1,0:T(8,128)(2,1)} %get-tuple-element.99), channel_id=1, source_target_pairs={{0,4},{4,0},{8,12},{12,8},{16,20},{20,16},{24,28},{28,24},{1,5},{5... | collective-permute-start | bytes 4718600 | tf_op jit(solution)/shard_map/ppermute | solution.py:617
  19.8 8.9 %collective-permute-start.8 = (bf16[128,1024]{1,0:T(8,128)(2,1)}, bf16[128,1024]{1,0:T(8,128)(2,1)S(1)}, u32[]{:S(2)}, u32[]{:S(2)}) collective-permute-start(bf16[128,1024]{1,0:T(8,128)(2,1)} %get-tuple-element.95), channel_id=1, source_target_pairs={{0,8},{4,12},{8,0},{12,4},{16,24},{20,28},{24,16},{28,20},{1,9},{5... | collective-permute-start | bytes 786440 | tf_op jit(solution)/shard_map/ppermute | solution.py:617
  21.3 14.9 %collective-permute-start.9 = (bf16[128,1024]{1,0:T(8,128)(2,1)}, bf16[128,1024]{1,0:T(8,128)(2,1)S(1)}, u32[]{:S(2)}, u32[]{:S(2)}) collective-permute-start(bf16[128,1024]{1,0:T(8,128)(2,1)} %get-tuple-element.96), channel_id=1, source_target_pairs={{0,16},{4,20},{8,24},{12,28},{16,0},{20,4},{24,8},{28,12},{1,17},{... | collective-permute-start | bytes 786440 | tf_op jit(solution)/shard_map/ppermute | solution.py:617
  22.9 15.9 %collective-permute-start.6 = (bf16[144,1024]{1,0:T(8,128)(2,1)S(1)}, bf16[144,1024]{1,0:T(8,128)(2,1)S(1)}, u32[]{:S(2)}, u32[]{:S(2)}) collective-permute-start(bf16[144,1024]{1,0:T(8,128)(2,1)S(1)} %pair.2.refs_0_), channel_id=1, source_target_pairs={{0,24},{4,28},{8,16},{12,20},{17,9},{21,13},{25,1},{29,5}} | collective-permute-start | bytes 884744 | tf_op jit(solution)/shard_map/ppermute | solution.py:752
  23.5 15.2 %collective-permute-start.5 = (bf16[144,1024]{1,0:T(8,128)(2,1)S(1)}, bf16[144,1024]{1,0:T(8,128)(2,1)S(1)}, u32[]{:S(2)}, u32[]{:S(2)}) collective-permute-start(bf16[144,1024]{1,0:T(8,128)(2,1)S(1)} %pair.2.refs_0_), channel_id=1, source_target_pairs={{0,16},{4,20},{8,24},{12,28},{17,1},{21,5},{25,9},{29,13}} | collective-permute-start | bytes 884744 | tf_op jit(solution)/shard_map/ppermute | solution.py:752
  28.7 7.5 %copy-start.8 = (bf16[128,1024]{1,0:T(8,128)(2,1)}, bf16[128,1024]{1,0:T(8,128)(2,1)S(1)}, u32[]{:S(2)}) copy-start(bf16[128,1024]{1,0:T(8,128)(2,1)S(1)} %collective-permute-done.8.refs_0_.refs_14_.refs_5_) | copy-start | bytes 786436
  28.7 10.1 %collective-permute-start.4 = (bf16[144,1024]{1,0:T(8,128)(2,1)S(1)}, bf16[144,1024]{1,0:T(8,128)(2,1)S(1)}, u32[]{:S(2)}, u32[]{:S(2)}) collective-permute-start(bf16[144,1024]{1,0:T(8,128)(2,1)S(1)} %pair.2.refs_0_), channel_id=1, source_target_pairs={{0,8},{4,12},{16,24},{20,28},{9,1},{13,5},{25,17},{29,21}} | collective-permute-start | bytes 884744 | tf_op jit(solution)/shard_map/ppermute | solution.py:752
  36.2 6.0 %copy-start.1 = (bf16[512,1024]{1,0:T(8,128)(2,1)S(1)}, bf16[512,1024]{1,0:T(8,128)(2,1)}, u32[]{:S(2)}) copy-start(bf16[512,1024]{1,0:T(8,128)(2,1)} %refs_0_.3) | copy-start | bytes 3145732
  36.2 0.7 copy-start.9
  38.7 2.1 %collective-permute-start.11 = (bf16[256,1024]{1,0:T(8,128)(2,1)}, bf16[256,1024]{1,0:T(8,128)(2,1)S(1)}, u32[]{:S(2)}, u32[]{:S(2)}) collective-permute-start(bf16[256,1024]{1,0:T(8,128)(2,1)} %stack.40), channel_id=1, source_target_pairs={{0,4},{4,0},{8,12},{12,8},{16,20},{20,16},{24,28},{28,24},{1,5},{5... | collective-permute-start | bytes 1572872 | tf_op jit(solution)/shard_map/ppermute | solution.py:617
  39.7 0.7 collective-permute-start.7
  40.9 0.8 copy-start.7
  40.9 1.3 copy-start.4
  48.2 8.2 %collective-permute-start.16 = (bf16[128,1024]{1,0:T(8,128)(2,1)S(1)}, bf16[128,1024]{1,0:T(8,128)(2,1)S(1)}, u32[]{:S(2)}, u32[]{:S(2)}) collective-permute-start(bf16[128,1024]{1,0:T(8,128)(2,1)S(1)} %get-tuple-element.106), channel_id=1, source_target_pairs={{0,1},{4,5},{8,9},{12,13},{16,17},{20,21},{24,25},{28,29}} | collective-permute-start | bytes 786440 | tf_op jit(solution)/shard_map/ppermute | solution.py:917
  48.9 8.9 %collective-permute-start.12 = (bf16[128,1024]{1,0:T(8,128)(2,1)S(1)}, bf16[128,1024]{1,0:T(8,128)(2,1)S(1)}, u32[]{:S(2)}, u32[]{:S(2)}) collective-permute-start(bf16[128,1024]{1,0:T(8,128)(2,1)S(1)} %get-tuple-element.102), channel_id=1, source_target_pairs={{0,1},{4,5},{8,9},{12,13},{16,17},{20,21},{24,25},{28,29}} | collective-permute-start | bytes 786440 | tf_op jit(solution)/shard_map/ppermute | solution.py:917
  56.5 22.6 %collective-permute-start.17 = (bf16[128,1024]{1,0:T(8,128)(2,1)S(1)}, bf16[128,1024]{1,0:T(8,128)(2,1)S(1)}, u32[]{:S(2)}, u32[]{:S(2)}) collective-permute-start(bf16[128,1024]{1,0:T(8,128)(2,1)S(1)} %add_convert_fusion.1.refs_12_), channel_id=1, source_target_pairs={{0,1},{1,2},{4,5},{5,6},{8,9},{9,10},{12,13},{13,14},{16,17},{17,1... | collective-permute-start | bytes 786440 | tf_op jit(solution)/shard_map/ppermute | solution.py:917
  57.9 27.4 %collective-permute-start.13 = (bf16[128,1024]{1,0:T(8,128)(2,1)S(1)}, bf16[128,1024]{1,0:T(8,128)(2,1)S(1)}, u32[]{:S(2)}, u32[]{:S(2)}) collective-permute-start(bf16[128,1024]{1,0:T(8,128)(2,1)S(1)} %add_convert_fusion.3.refs_13_), channel_id=1, source_target_pairs={{0,1},{1,2},{4,5},{5,6},{8,9},{9,10},{12,13},{13,14},{16,17},{17,1... | collective-permute-start | bytes 786440 | tf_op jit(solution)/shard_map/ppermute | solution.py:917
  79.2 11.8 %collective-permute-start.18 = (bf16[128,1024]{1,0:T(8,128)(2,1)S(1)}, bf16[128,1024]{1,0:T(8,128)(2,1)S(1)}, u32[]{:S(2)}, u32[]{:S(2)}) collective-permute-start(bf16[128,1024]{1,0:T(8,128)(2,1)S(1)} %add_convert_fusion.refs_12_), channel_id=1, source_target_pairs={{1,2},{2,3},{5,6},{6,7},{9,10},{10,11},{13,14},{14,15},{17,18},{18... | collective-permute-start | bytes 786440 | tf_op jit(solution)/shard_map/ppermute | solution.py:917
  85.4 13.3 %copy-start.2 = (bf16[128,1024]{1,0:T(8,128)(2,1)}, bf16[128,1024]{1,0:T(8,128)(2,1)S(1)}, u32[]{:S(2)}) copy-start(bf16[128,1024]{1,0:T(8,128)(2,1)S(1)} %add_convert_fusion.2.refs_0_.refs_13_) | copy-start | bytes 786436
  85.4 11.3 %collective-permute-start.14 = (bf16[128,1024]{1,0:T(8,128)(2,1)S(1)}, bf16[128,1024]{1,0:T(8,128)(2,1)S(1)}, u32[]{:S(2)}, u32[]{:S(2)}) collective-permute-start(bf16[128,1024]{1,0:T(8,128)(2,1)S(1)} %add_convert_fusion.2.refs_0_.refs_13_), channel_id=1, source_target_pairs={{1,2},{2,3},{5,6},{6,7},{9,10},{10,11},{13,14},{14,15},{17,18},{18... | collective-permute-start | bytes 786440 | tf_op jit(solution)/shard_map/ppermute | solution.py:917
  87.4 17.0 %collective-permute-start.15 = (bf16[128,1024]{1,0:T(8,128)(2,1)S(1)}, bf16[128,1024]{1,0:T(8,128)(2,1)S(1)}, u32[]{:S(2)}, u32[]{:S(2)}) collective-permute-start(bf16[128,1024]{1,0:T(8,128)(2,1)S(1)} %add_convert_fusion.2.refs_0_.refs_13_), channel_id=1, source_target_pairs={{1,3},{5,7},{9,11},{13,15},{17,19},{21,23},{25,27},{29,31}} | collective-permute-start | bytes 786440 | tf_op jit(solution)/shard_map/ppermute | solution.py:919
  91.0 13.4 %collective-permute-start.19 = (bf16[128,1024]{1,0:T(8,128)(2,1)S(1)}, bf16[128,1024]{1,0:T(8,128)(2,1)S(1)}, u32[]{:S(2)}, u32[]{:S(2)}) collective-permute-start(bf16[128,1024]{1,0:T(8,128)(2,1)S(1)} %collective-permute-done.18), channel_id=1, source_target_pairs={{2,3},{6,7},{10,11},{14,15},{18,19},{22,23},{26,27},{30,31}} | collective-permute-start | bytes 786440 | tf_op jit(solution)/shard_map/ppermute | solution.py:917
  96.8 7.6 %collective-permute-start.20 = (bf16[16,1024]{1,0:T(8,128)(2,1)S(1)}, bf16[16,1024]{1,0:T(8,128)(2,1)S(1)}, u32[]{:S(2)}, u32[]{:S(2)}) collective-permute-start(bf16[16,1024]{1,0:T(8,128)(2,1)S(1)} %slice_select_fusion), channel_id=1, source_target_pairs={{2,6},{6,10},{10,14},{14,18},{18,22},{22,26},{26,30},{7,3},{11,7},... | collective-permute-start | bytes 98312 | tf_op jit(solution)/shard_map/ppermute | solution.py:822
  114.1 5.2 %collective-permute-start.21 = (bf16[144,2048]{1,0:T(8,128)(2,1)S(1)}, bf16[144,2048]{1,0:T(8,128)(2,1)S(1)}, u32[]{:S(2)}, u32[]{:S(2)}) collective-permute-start(bf16[144,2048]{1,0:T(8,128)(2,1)S(1)} %get-tuple-element.120.mine), channel_id=1, source_target_pairs={{2,6},{6,2},{10,14},{14,10},{18,22},{22,18},{26,30},{30,26},{3,7},... | collective-permute-start | bytes 1769480 | tf_op jit(solution)/shard_map/ppermute | solution.py:743
  120.0 12.2 %collective-permute-start.24 = (bf16[144,1024]{1,0:T(8,128)(2,1)S(1)}, bf16[144,1024]{1,0:T(8,128)(2,1)S(1)}, u32[]{:S(2)}, u32[]{:S(2)}) collective-permute-start(bf16[144,1024]{1,0:T(8,128)(2,1)S(1)} %pair.3.refs_0_), channel_id=1, source_target_pairs={{2,26},{6,30},{10,18},{14,22},{19,11},{23,15},{27,3},{31,7}} | collective-permute-start | bytes 884744 | tf_op jit(solution)/shard_map/ppermute | solution.py:752
  121.3 17.1 %collective-permute-start.23 = (bf16[144,1024]{1,0:T(8,128)(2,1)S(1)}, bf16[144,1024]{1,0:T(8,128)(2,1)S(1)}, u32[]{:S(2)}, u32[]{:S(2)}) collective-permute-start(bf16[144,1024]{1,0:T(8,128)(2,1)S(1)} %pair.3.refs_0_), channel_id=1, source_target_pairs={{2,18},{6,22},{10,26},{14,30},{19,3},{23,7},{27,11},{31,15}} | collective-permute-start | bytes 884744 | tf_op jit(solution)/shard_map/ppermute | solution.py:752
  122.6 15.8 %collective-permute-start.22 = (bf16[144,1024]{1,0:T(8,128)(2,1)S(1)}, bf16[144,1024]{1,0:T(8,128)(2,1)S(1)}, u32[]{:S(2)}, u32[]{:S(2)}) collective-permute-start(bf16[144,1024]{1,0:T(8,128)(2,1)S(1)} %pair.3.refs_0_), channel_id=1, source_target_pairs={{2,10},{6,14},{18,26},{22,30},{11,3},{15,7},{27,19},{31,23}} | collective-permute-start | bytes 884744 | tf_op jit(solution)/shard_map/ppermute | solution.py:752
  131.0 11.8 %copy-start = (bf16[512,1024]{1,0:T(8,128)(2,1)S(1)}, bf16[512,1024]{1,0:T(8,128)(2,1)}, u32[]{:S(2)}) copy-start(bf16[512,1024]{1,0:T(8,128)(2,1)} %pad_maximum_fusion.rows.refs_0_) | copy-start | bytes 3145732
  139.4 3.4 %collective-permute-start.25 = (bf16[128,1024]{1,0:T(8,128)(2,1)S(1)}, bf16[128,1024]{1,0:T(8,128)(2,1)S(1)}, u32[]{:S(2)}, u32[]{:S(2)}) collective-permute-start(bf16[128,1024]{1,0:T(8,128)(2,1)S(1)} %merge.3.refs_6_), channel_id=1, source_target_pairs={{2,6},{6,2},{10,14},{14,10},{18,22},{22,18},{26,30},{30,26},{3,7},... | collective-permute-start | bytes 786440 | tf_op jit(solution)/shard_map/ppermute | solution.py:743
  142.8 9.6 %copy-start.3 = (bf16[128,1024]{1,0:T(8,128)(2,1)S(1)}, bf16[128,1024]{1,0:T(8,128)(2,1)}, u32[]{:S(2)}) copy-start(bf16[128,1024]{1,0:T(8,128)(2,1)} %copy-done.2) | copy-start | bytes 786436
  146.5 18.0 %collective-permute-start.28 = (bf16[128,1024]{1,0:T(8,128)(2,1)S(1)}, bf16[128,1024]{1,0:T(8,128)(2,1)S(1)}, u32[]{:S(2)}, u32[]{:S(2)}) collective-permute-start(bf16[128,1024]{1,0:T(8,128)(2,1)S(1)} %get-tuple-element.140.sent), channel_id=1, source_target_pairs={{2,3},{3,2},{1,0},{6,7},{7,6},{5,4},{10,11},{11,10},{9,8},{14,15},... | collective-permute-start | bytes 786440 | tf_op jit(solution)/shard_map/ppermute | solution.py:936
  148.5 14.7 %collective-permute-start.29 = (bf16[128,1024]{1,0:T(8,128)(2,1)S(1)}, bf16[128,1024]{1,0:T(8,128)(2,1)S(1)}, u32[]{:S(2)}, u32[]{:S(2)}) collective-permute-start(bf16[128,1024]{1,0:T(8,128)(2,1)S(1)} %get-tuple-element.142.sent), channel_id=1, source_target_pairs={{2,3},{3,2},{1,0},{6,7},{7,6},{5,4},{10,11},{11,10},{9,8},{14,15},... | collective-permute-start | bytes 786440 | tf_op jit(solution)/shard_map/ppermute | solution.py:936
  156.8 12.0 %collective-permute-start.27 = (bf16[128,1024]{1,0:T(8,128)(2,1)S(1)}, bf16[128,1024]{1,0:T(8,128)(2,1)S(1)}, u32[]{:S(2)}, u32[]{:S(2)}) collective-permute-start(bf16[128,1024]{1,0:T(8,128)(2,1)S(1)} %get-tuple-element.138.sent), channel_id=1, source_target_pairs={{2,3},{3,2},{1,0},{6,7},{7,6},{5,4},{10,11},{11,10},{9,8},{14,15},... | collective-permute-start | bytes 786440 | tf_op jit(solution)/shard_map/ppermute | solution.py:936
  158.8 14.8 %collective-permute-start.26 = (bf16[128,1024]{1,0:T(8,128)(2,1)S(1)}, bf16[128,1024]{1,0:T(8,128)(2,1)S(1)}, u32[]{:S(2)}, u32[]{:S(2)}) collective-permute-start(bf16[128,1024]{1,0:T(8,128)(2,1)S(1)} %get-tuple-element.136.sent), channel_id=1, source_target_pairs={{2,3},{3,2},{1,0},{6,7},{7,6},{5,4},{10,11},{11,10},{9,8},{14,15},... | collective-permute-start | bytes 786440 | tf_op jit(solution)/shard_map/ppermute | solution.py:936
where the time goes:
time: 176 us; the launch traced here: 175 us
  Pallas kernels  71.7 us (41%)
  waiting for transfers between devices  55 us (31%)
  starting transfers between devices  43.3 us (25%)
  other arithmetic  2.28 us (1%)
  local copies, waits for them, and re-layouts  2.14 us (1%)
    ppermute x7, waiting for transfers between devices, per_device(): received.append(lax.ppermute(value, 'section', pairs))  31.5 us
    pallas_call x4, Pallas kernels, finish(): pl.pallas_call(functools.partial(finish_kernel, plan, shard_rows, members...  20.7 us
    pallas_call x2, Pallas kernels, prep(): pl.pallas_call(prep_kernel, grid_spec=grid_spec, out_shape=[kept((length,...  19.6 us
    pallas_call x2, Pallas kernels, mid(): pl.pallas_call(mid_kernel, grid=(steps,), in_specs=[whole_block((length,...  12.7 us
    ppermute x4, starting transfers between devices, per_device(): lax.ppermute(terms[index], 'section', [(low, high), (high, low), (1, 0)])  11.7 us
    ppermute x7, starting transfers between devices, per_device(): received.append(lax.ppermute(value, 'section', pairs))  9.25 us
    ppermute x6, waiting for transfers between devices, forward(): return lax.ppermute(value, ('seq', 'section'), pairs)  7.43 us
    ppermute x6, starting transfers between devices, forward(): return lax.ppermute(value, ('seq', 'section'), pairs)  7.01 us
  transfers between devices with their start and end apart: 30, of which 15 were waited for; matrix products, arithmetic and copies ran while one was open for 0% of the time, Pallas kernels for 27%

commit v1 on v0

--- a/solution.py
+++ b/solution.py
@@ -429,7 +429,7 @@
             flops=2 * length * features * inner, bytes_accessed=12 * 2**20, transcendentals=0
         ),
         name="prep",
-    )(info, far(rows), halo, gain, main, side, conv, conv, bias, decay, spread)
+    )(info, place(rows), halo, gain, main, side, conv, conv, bias, decay, spread)
 
 
 def mid(normed, main, x, b, c_rows, cumulative, shifted, params, inner, resident=False):

time: 176 us -> 173 us (0.983)
  no operation moved by 1% of the time
where the time goes in v1:
time: 173 us
  Pallas kernels  70.4 us (41%)
  waiting for transfers between devices  55 us (32%)
  starting transfers between devices  43.2 us (25%)
  local copies, waits for them, and re-layouts  2.14 us (1%)
    ppermute x7, waiting for transfers between devices, per_device(): received.append(lax.ppermute(value, 'section', pairs))  31.5 us
    pallas_call x4, Pallas kernels, finish(): pl.pallas_call(functools.partial(finish_kernel, plan, shard_rows, members...  20.7 us
    pallas_call x2, Pallas kernels, prep(): pl.pallas_call(prep_kernel, grid_spec=grid_spec, out_shape=[kept((length,...  18.3 us
    pallas_call x2, Pallas kernels, mid(): pl.pallas_call(mid_kernel, grid=(steps,), in_specs=[whole_block((length,...  12.7 us
    ppermute x4, starting transfers between devices, per_device(): lax.ppermute(terms[index], 'section', [(low, high), (high, low), (1, 0)])  11.7 us
    ppermute x7, starting transfers between devices, per_device(): received.append(lax.ppermute(value, 'section', pairs))  9.25 us
    ppermute x6, waiting for transfers between devices, forward(): return lax.ppermute(value, ('seq', 'section'), pairs)  7.42 us
    ppermute x6, starting transfers between devices, forward(): return lax.ppermute(value, ('seq', 'section'), pairs)  7.02 us
  transfers between devices with their start and end apart: 30, of which 15 were waited for; matrix products, arithmetic and copies ran while one was open for 0% of the time, Pallas kernels for 27%

profile of v1, /device:TPU:20, one launch (start us, length us, event | category | flops | bytes accessed | tf_op | source)
XLA Modules:
  0.0 172.6 jit_solution(15506442672379534069)
XLA Ops:
  2.0 1.5 collective-permute-start.1
  3.6 10.9 %prep.2 = (bf16[512,1024]{1,0:T(8,128)(2,1)S(1)}, bf16[512,2048]{1,0:T(8,128)(2,1)S(1)}, bf16[512,128]{1,0:T(8,128)(2,1)S(1)}, bf16[512,128]{1,0:T(8,128)(2,1)S(...) custom-call(s32[7]{0:T(128)S(1)} %stack.37.info, ...), custom_call_target="tpu_custom_call" | custom-call | flops 2147483648 | bytes 12582912 | tf_op jit(solution)/shard_map/prep/pallas_call | solution.py:411
  14.6 0.8 collective-permute-done.2.refs_0_.refs_4_.refs_13_
  17.0 2.7 %stack.39 = (bf16[128,1024]{1,0:T(8,128)(2,1)}, bf16[128,1024]{1,0:T(8,128)(2,1)}, bf16[768,1024]{1,0:T(8,128)(2,1)}) custom-call(bf16[256,1024]{1,0:T(8,128)(2,1)} %copy-done.8, bf16[256,1024]{1,0:T(8,128)(2,1)} %copy-done.9, bf16[256,1024]{1,0:T(8,128)(2,1)} %bitcast.11, bf16[256,1024]{1,0:T(8,128)(2,1)} %copy-done.9, bf16[256,1024]{1,0:T(8,128)(2,1)} %copy-done.8), custom_call_target="tpu_custom_call" | custom-call | flops 1000000 | bytes 1000000 | tf_op jit(solution)/shard_map/stack/pallas_call | solution.py:601
  19.8 1.6 collective-permute-start.8
  21.3 1.5 collective-permute-start.9
  24.2 4.5 %collective-permute-done.8.refs_0_.refs_14_.refs_5_ = bf16[128,1024]{1,0:T(8,128)(2,1)S(1)} collective-permute-done((bf16[128,1024]{1,0:T(8,128)(2,1)}, bf16[128,1024]{1,0:T(8,128)(2,1)S(1)}, u32[]{:S(2)}, u32[]{:S(2)}) %collective-permute-start.8) | collective-permute-done | bytes 262176 | tf_op jit(solution)/shard_map/ppermute | solution.py:617
  29.4 6.8 %mid.2 = (f32[512,2048]{1,0:T(8,128)S(1)}, bf16[512,2048]{1,0:T(8,128)(2,1)S(1)}) custom-call(bf16[512,1024]{1,0:T(8,128)(2,1)S(1)} %get-tuple-element.79.normed, bf16[1,1024,4096]{2,1,0:T(8,128)(2,1)} %refs_1_.1, bf16[512,2048]{1,0:T(8,128)(2,1)S(1)} %get-tuple-element.80.x, bf16[512,128]{1,0:T(8,128)(2,1)S(1)} %get-tuple-element.81.b, ...), custom_call_target="tpu_custom_call" | custom-call | flops 2147483648 | bytes 12582912 | tf_op jit(solution)/shard_map/mid/pallas_call | solution.py:443
  36.9 1.8 %stack.40 = bf16[256,1024]{1,0:T(8,128)(2,1)} custom-call(bf16[128,1024]{1,0:T(8,128)(2,1)} %copy-done.11, bf16[128,1024]{1,0:T(8,128)(2,1)} %copy-done.12), custom_call_target="tpu_custom_call" | custom-call | flops 1000000 | bytes 1000000 | tf_op jit(solution)/shard_map/stack/pallas_call | solution.py:601
  38.7 0.9 merge.2.refs_6_
  42.2 6.0 %finish.5 = (bf16[128,1024]{1,0:T(8,128)(2,1)S(1)}, bf16[128,1024]{1,0:T(8,128)(2,1)S(1)}, f32[128,1024]{1,0:T(8,128)S(1)}, f32[128,1024]{1,0:T(8,128)S(1)}) custom-call(s32[7]{0:T(128)S(1)} %stack.37.info, bf16[512,1024]{1,0:T(8,128)(2,1)S(1)} %copy-done, f32[512,2048]{1,0:T(8,128)S(1)} %get-tuple-element.85.refs_1_, ...), custom_call_target="tpu_custom_call" | custom-call | flops 1073741824 | bytes 8388608 | tf_op jit(solution)/shard_map/finish/pallas_call | solution.py:504
  48.9 0.9 collective-permute-start.12
  49.7 6.6 %finish.4 = (bf16[128,1024]{1,0:T(8,128)(2,1)S(1)}, bf16[128,1024]{1,0:T(8,128)(2,1)S(1)}, f32[128,1024]{1,0:T(8,128)S(1)}, f32[128,1024]{1,0:T(8,128)S(1)}) custom-call(s32[7]{0:T(128)S(1)} %stack.37.info, bf16[512,1024]{1,0:T(8,128)(2,1)S(1)} %copy-done, f32[512,2048]{1,0:T(8,128)S(1)} %get-tuple-element.85.refs_1_, ...), custom_call_target="tpu_custom_call" | custom-call | flops 1073741824 | bytes 8388608 | tf_op jit(solution)/shard_map/finish/pallas_call | solution.py:504
  56.5 1.3 collective-permute-start.17
  57.9 1.3 collective-permute-start.13
  59.2 19.9 %collective-permute-done.17 = bf16[128,1024]{1,0:T(8,128)(2,1)S(1)} collective-permute-done((bf16[128,1024]{1,0:T(8,128)(2,1)S(1)}, bf16[128,1024]{1,0:T(8,128)(2,1)S(1)}, u32[]{:S(2)}, u32[]{:S(2)}) %collective-permute-start.17) | collective-permute-done | bytes 262176 | tf_op jit(solution)/shard_map/ppermute | solution.py:917
  79.2 1.9 %collective-permute-start.18 = (bf16[128,1024]{1,0:T(8,128)(2,1)S(1)}, bf16[128,1024]{1,0:T(8,128)(2,1)S(1)}, u32[]{:S(2)}, u32[]{:S(2)}) collective-permute-start(bf16[128,1024]{1,0:T(8,128)(2,1)S(1)} %add_convert_fusion.refs_12_), channel_id=1, source_target_pairs={{1,2},{2,3},{5,6},{6,7},{9,10},{10,11},{13,14},{14,15},{17,18},{18... | collective-permute-start | bytes 786440 | tf_op jit(solution)/shard_map/ppermute | solution.py:917
  81.1 4.2 %collective-permute-done.13 = bf16[128,1024]{1,0:T(8,128)(2,1)S(1)} collective-permute-done((bf16[128,1024]{1,0:T(8,128)(2,1)S(1)}, bf16[128,1024]{1,0:T(8,128)(2,1)S(1)}, u32[]{:S(2)}, u32[]{:S(2)}) %collective-permute-start.13) | collective-permute-done | bytes 262176 | tf_op jit(solution)/shard_map/ppermute | solution.py:917
  85.4 1.9 %collective-permute-start.14 = (bf16[128,1024]{1,0:T(8,128)(2,1)S(1)}, bf16[128,1024]{1,0:T(8,128)(2,1)S(1)}, u32[]{:S(2)}, u32[]{:S(2)}) collective-permute-start(bf16[128,1024]{1,0:T(8,128)(2,1)S(1)} %add_convert_fusion.2.refs_0_.refs_13_), channel_id=1, source_target_pairs={{1,2},{2,3},{5,6},{6,7},{9,10},{10,11},{13,14},{14,15},{17,18},{18... | collective-permute-start | bytes 786440 | tf_op jit(solution)/shard_map/ppermute | solution.py:917
  88.0 2.9 %collective-permute-done.18 = bf16[128,1024]{1,0:T(8,128)(2,1)S(1)} collective-permute-done((bf16[128,1024]{1,0:T(8,128)(2,1)S(1)}, bf16[128,1024]{1,0:T(8,128)(2,1)S(1)}, u32[]{:S(2)}, u32[]{:S(2)}) %collective-permute-start.18) | collective-permute-done | bytes 262176 | tf_op jit(solution)/shard_map/ppermute | solution.py:917
  91.0 1.3 collective-permute-start.19
  92.3 4.5 %collective-permute-done.14 = bf16[128,1024]{1,0:T(8,128)(2,1)S(1)} collective-permute-done((bf16[128,1024]{1,0:T(8,128)(2,1)S(1)}, bf16[128,1024]{1,0:T(8,128)(2,1)S(1)}, u32[]{:S(2)}, u32[]{:S(2)}) %collective-permute-start.14) | collective-permute-done | bytes 262176 | tf_op jit(solution)/shard_map/ppermute | solution.py:917
  96.8 1.9 %collective-permute-start.20 = (bf16[16,1024]{1,0:T(8,128)(2,1)S(1)}, bf16[16,1024]{1,0:T(8,128)(2,1)S(1)}, u32[]{:S(2)}, u32[]{:S(2)}) collective-permute-start(bf16[16,1024]{1,0:T(8,128)(2,1)S(1)} %slice_select_fusion), channel_id=1, source_target_pairs={{2,6},{6,10},{10,14},{14,18},{18,22},{22,26},{26,30},{7,3},{11,7},... | collective-permute-start | bytes 98312 | tf_op jit(solution)/shard_map/ppermute | solution.py:822
  98.7 5.6 %hold.1 = (bf16[1,1024,4096]{2,1,0:T(8,128)(2,1)S(1)}, bf16[2048,1024]{1,0:T(8,128)(2,1)S(1)}, f32[1,1024]{1,0:T(1,128)S(1)}, bf16[1,288,1024]{2,1,0:T(8,128)(2,...) custom-call(s32[7]{0:T(128)S(1)} %stack.37.info, ...), custom_call_target="tpu_custom_call" | custom-call | flops 1000000 | bytes 25165824 | tf_op jit(solution)/shard_map/hold/pallas_call | solution.py:548
  104.5 7.3 %prep.3 = (bf16[512,1024]{1,0:T(8,128)(2,1)S(1)}, bf16[512,2048]{1,0:T(8,128)(2,1)S(1)}, bf16[512,128]{1,0:T(8,128)(2,1)S(1)}, bf16[512,128]{1,0:T(8,128)(2,1)S(...) custom-call(s32[7]{0:T(128)S(1)} %stack.37.info, ...), custom_call_target="tpu_custom_call" | custom-call | flops 2147483648 | bytes 12582912 | tf_op jit(solution)/shard_map/prep/pallas_call | solution.py:411
  111.9 3.6 %collective-permute-start.21 = (bf16[144,2048]{1,0:T(8,128)(2,1)S(1)}, bf16[144,2048]{1,0:T(8,128)(2,1)S(1)}, u32[]{:S(2)}, u32[]{:S(2)}) collective-permute-start(bf16[144,2048]{1,0:T(8,128)(2,1)S(1)} %get-tuple-element.120.mine), channel_id=1, source_target_pairs={{2,6},{6,2},{10,14},{14,10},{18,22},{22,18},{26,30},{30,26},{3,7},... | collective-permute-start | bytes 1769480 | tf_op jit(solution)/shard_map/ppermute | solution.py:743
  115.4 1.6 collective-permute-done.21.partner.refs_8_
  117.7 1.3 collective-permute-start.24
  119.0 1.3 collective-permute-start.23
  120.3 2.4 %collective-permute-start.22 = (bf16[144,1024]{1,0:T(8,128)(2,1)S(1)}, bf16[144,1024]{1,0:T(8,128)(2,1)S(1)}, u32[]{:S(2)}, u32[]{:S(2)}) collective-permute-start(bf16[144,1024]{1,0:T(8,128)(2,1)S(1)} %pair.3.refs_0_), channel_id=1, source_target_pairs={{2,10},{6,14},{18,26},{22,30},{11,3},{15,7},{27,19},{31,23}} | collective-permute-start | bytes 884744 | tf_op jit(solution)/shard_map/ppermute | solution.py:752
  122.8 5.9 %mid.3 = (f32[512,2048]{1,0:T(8,128)S(1)}, bf16[512,2048]{1,0:T(8,128)(2,1)S(1)}) custom-call(bf16[512,1024]{1,0:T(8,128)(2,1)S(1)} %get-tuple-element.121.normed, bf16[1,1024,4096]{2,1,0:T(8,128)(2,1)S(1)} %get-tuple-element.113.wide.gate_weight, bf16[512,2048]{1,0:T(8,128)(2,1)S(1)} %get-tuple-element.122.x, bf16[512,128]{1,0:T(8,128)(2,1)S(1)} %get-tuple-element.123.b, ...), custom_call_target="tpu_custom_call" | custom-call | flops 2147483648 | bytes 12582912 | tf_op jit(solution)/shard_map/mid/pallas_call | solution.py:443
  128.7 1.2 collective-permute-done.24.refs_3_
  129.9 6.2 %collective-permute-done.23.refs_2_ = bf16[144,1024]{1,0:T(8,128)(2,1)S(1)} collective-permute-done((bf16[144,1024]{1,0:T(8,128)(2,1)S(1)}, bf16[144,1024]{1,0:T(8,128)(2,1)S(1)}, u32[]{:S(2)}, u32[]{:S(2)}) %collective-permute-start.23) | collective-permute-done | bytes 294944 | tf_op jit(solution)/shard_map/ppermute | solution.py:752
  136.1 0.9 merge.3.refs_6_
  137.1 2.0 %collective-permute-start.25 = (bf16[128,1024]{1,0:T(8,128)(2,1)S(1)}, bf16[128,1024]{1,0:T(8,128)(2,1)S(1)}, u32[]{:S(2)}, u32[]{:S(2)}) collective-permute-start(bf16[128,1024]{1,0:T(8,128)(2,1)S(1)} %merge.3.refs_6_), channel_id=1, source_target_pairs={{2,6},{6,2},{10,14},{14,10},{18,22},{22,18},{26,30},{30,26},{3,7},... | collective-permute-start | bytes 786440 | tf_op jit(solution)/shard_map/ppermute | solution.py:743
  139.1 1.5 collective-permute-done.25.refs_7_
  140.5 3.7 %finish.7 = (bf16[128,1024]{1,0:T(8,128)(2,1)S(1)}, bf16[128,1024]{1,0:T(8,128)(2,1)S(1)}, f32[128,1024]{1,0:T(8,128)S(1)}, f32[128,1024]{1,0:T(8,128)S(1)}) custom-call(s32[7]{0:T(128)S(1)} %stack.37.info, bf16[512,1024]{1,0:T(8,128)(2,1)S(1)} %pad_maximum_fusion.rows.refs_0_, f32[512,2048]{1,0:T(8,128)S(1)} %get-tuple-element.128.refs_1_, ...), custom_call_target="tpu_custom_call" | custom-call | flops 1073741824 | bytes 8388608 | tf_op jit(solution)/shard_map/finish/pallas_call | solution.py:504
  144.2 2.0 %collective-permute-start.28 = (bf16[128,1024]{1,0:T(8,128)(2,1)S(1)}, bf16[128,1024]{1,0:T(8,128)(2,1)S(1)}, u32[]{:S(2)}, u32[]{:S(2)}) collective-permute-start(bf16[128,1024]{1,0:T(8,128)(2,1)S(1)} %get-tuple-element.140.sent), channel_id=1, source_target_pairs={{2,3},{3,2},{1,0},{6,7},{7,6},{5,4},{10,11},{11,10},{9,8},{14,15},... | collective-permute-start | bytes 786440 | tf_op jit(solution)/shard_map/ppermute | solution.py:936
  146.2 3.9 %collective-permute-start.29 = (bf16[128,1024]{1,0:T(8,128)(2,1)S(1)}, bf16[128,1024]{1,0:T(8,128)(2,1)S(1)}, u32[]{:S(2)}, u32[]{:S(2)}) collective-permute-start(bf16[128,1024]{1,0:T(8,128)(2,1)S(1)} %get-tuple-element.142.sent), channel_id=1, source_target_pairs={{2,3},{3,2},{1,0},{6,7},{7,6},{5,4},{10,11},{11,10},{9,8},{14,15},... | collective-permute-start | bytes 786440 | tf_op jit(solution)/shard_map/ppermute | solution.py:936
  150.1 4.4 %finish.6 = (bf16[128,1024]{1,0:T(8,128)(2,1)S(1)}, bf16[128,1024]{1,0:T(8,128)(2,1)S(1)}, f32[128,1024]{1,0:T(8,128)S(1)}, f32[128,1024]{1,0:T(8,128)S(1)}) custom-call(s32[7]{0:T(128)S(1)} %stack.37.info, bf16[512,1024]{1,0:T(8,128)(2,1)S(1)} %pad_maximum_fusion.rows.refs_0_, f32[512,2048]{1,0:T(8,128)S(1)} %get-tuple-element.128.refs_1_, ...), custom_call_target="tpu_custom_call" | custom-call | flops 1073741824 | bytes 8388608 | tf_op jit(solution)/shard_map/finish/pallas_call | solution.py:504
  154.6 2.0 %collective-permute-start.27 = (bf16[128,1024]{1,0:T(8,128)(2,1)S(1)}, bf16[128,1024]{1,0:T(8,128)(2,1)S(1)}, u32[]{:S(2)}, u32[]{:S(2)}) collective-permute-start(bf16[128,1024]{1,0:T(8,128)(2,1)S(1)} %get-tuple-element.138.sent), channel_id=1, source_target_pairs={{2,3},{3,2},{1,0},{6,7},{7,6},{5,4},{10,11},{11,10},{9,8},{14,15},... | collective-permute-start | bytes 786440 | tf_op jit(solution)/shard_map/ppermute | solution.py:936
  156.5 3.9 %collective-permute-start.26 = (bf16[128,1024]{1,0:T(8,128)(2,1)S(1)}, bf16[128,1024]{1,0:T(8,128)(2,1)S(1)}, u32[]{:S(2)}, u32[]{:S(2)}) collective-permute-start(bf16[128,1024]{1,0:T(8,128)(2,1)S(1)} %get-tuple-element.136.sent), channel_id=1, source_target_pairs={{2,3},{3,2},{1,0},{6,7},{7,6},{5,4},{10,11},{11,10},{9,8},{14,15},... | collective-permute-start | bytes 786440 | tf_op jit(solution)/shard_map/ppermute | solution.py:936
  160.9 1.3 settle.4.rest_0_
  162.2 1.3 settle.5.rest_0_
  163.5 3.0 %collective-permute-done.27.other = bf16[128,1024]{1,0:T(8,128)(2,1)S(1)} collective-permute-done((bf16[128,1024]{1,0:T(8,128)(2,1)S(1)}, bf16[128,1024]{1,0:T(8,128)(2,1)S(1)}, u32[]{:S(2)}, u32[]{:S(2)}) %collective-permute-start.27) | collective-permute-done | bytes 262176 | tf_op jit(solution)/shard_map/ppermute | solution.py:936
  166.5 1.3 settle.6.rest_0_
  167.8 3.5 %collective-permute-done.26.other = bf16[128,1024]{1,0:T(8,128)(2,1)S(1)} collective-permute-done((bf16[128,1024]{1,0:T(8,128)(2,1)S(1)}, bf16[128,1024]{1,0:T(8,128)(2,1)S(1)}, u32[]{:S(2)}, u32[]{:S(2)}) %collective-permute-start.26) | collective-permute-done | bytes 262176 | tf_op jit(solution)/shard_map/ppermute | solution.py:936
  171.3 1.3 settle.7
  (68 shorter events, 12.0 us)
Async XLA Ops:
  0.8 0.7 collective-permute-start
  1.5 13.9 %collective-permute-start.2 = (bf16[256,1024]{1,0:T(8,128)(2,1)}, bf16[256,1024]{1,0:T(8,128)(2,1)S(1)}, u32[]{:S(2)}, u32[]{:S(2)}) collective-permute-start(bf16[256,1024]{1,0:T(8,128)(2,1)} %bitcast.9), channel_id=1, source_target_pairs={{0,16},{4,20},{8,24},{12,28},{16,0},{20,4},{24,8},{28,12},{1,17},{... | collective-permute-start | bytes 1572872 | tf_op jit(solution)/shard_map/ppermute | solution.py:617
  2.0 13.6 %collective-permute-start.1 = (bf16[256,1024]{1,0:T(8,128)(2,1)}, bf16[256,1024]{1,0:T(8,128)(2,1)S(1)}, u32[]{:S(2)}, u32[]{:S(2)}) collective-permute-start(bf16[256,1024]{1,0:T(8,128)(2,1)} %bitcast.10), channel_id=1, source_target_pairs={{0,8},{4,12},{8,0},{12,4},{16,24},{20,28},{24,16},{28,20},{1,9},{5... | collective-permute-start | bytes 1572872 | tf_op jit(solution)/shard_map/ppermute | solution.py:617
  15.4 1.6 copy-start.8
  15.6 1.4 copy-start.9
  15.6 0.7 collective-permute-start.3
  19.8 21.1 %collective-permute-start.10 = (bf16[768,1024]{1,0:T(8,128)(2,1)}, bf16[768,1024]{1,0:T(8,128)(2,1)S(1)}, u32[]{:S(2)}, u32[]{:S(2)}) collective-permute-start(bf16[768,1024]{1,0:T(8,128)(2,1)} %get-tuple-element.99), channel_id=1, source_target_pairs={{0,4},{4,0},{8,12},{12,8},{16,20},{20,16},{24,28},{28,24},{1,5},{5... | collective-permute-start | bytes 4718600 | tf_op jit(solution)/shard_map/ppermute | solution.py:617
  19.8 8.9 %collective-permute-start.8 = (bf16[128,1024]{1,0:T(8,128)(2,1)}, bf16[128,1024]{1,0:T(8,128)(2,1)S(1)}, u32[]{:S(2)}, u32[]{:S(2)}) collective-permute-start(bf16[128,1024]{1,0:T(8,128)(2,1)} %get-tuple-element.95), channel_id=1, source_target_pairs={{0,8},{4,12},{8,0},{12,4},{16,24},{20,28},{24,16},{28,20},{1,9},{5... | collective-permute-start | bytes 786440 | tf_op jit(solution)/shard_map/ppermute | solution.py:617
  21.3 14.9 %collective-permute-start.9 = (bf16[128,1024]{1,0:T(8,128)(2,1)}, bf16[128,1024]{1,0:T(8,128)(2,1)S(1)}, u32[]{:S(2)}, u32[]{:S(2)}) collective-permute-start(bf16[128,1024]{1,0:T(8,128)(2,1)} %get-tuple-element.96), channel_id=1, source_target_pairs={{0,16},{4,20},{8,24},{12,28},{16,0},{20,4},{24,8},{28,12},{1,17},{... | collective-permute-start | bytes 786440 | tf_op jit(solution)/shard_map/ppermute | solution.py:617
  22.8 15.9 %collective-permute-start.6 = (bf16[144,1024]{1,0:T(8,128)(2,1)S(1)}, bf16[144,1024]{1,0:T(8,128)(2,1)S(1)}, u32[]{:S(2)}, u32[]{:S(2)}) collective-permute-start(bf16[144,1024]{1,0:T(8,128)(2,1)S(1)} %pair.2.refs_0_), channel_id=1, source_target_pairs={{0,24},{4,28},{8,16},{12,20},{17,9},{21,13},{25,1},{29,5}} | collective-permute-start | bytes 884744 | tf_op jit(solution)/shard_map/ppermute | solution.py:752
  23.5 15.2 %collective-permute-start.5 = (bf16[144,1024]{1,0:T(8,128)(2,1)S(1)}, bf16[144,1024]{1,0:T(8,128)(2,1)S(1)}, u32[]{:S(2)}, u32[]{:S(2)}) collective-permute-start(bf16[144,1024]{1,0:T(8,128)(2,1)S(1)} %pair.2.refs_0_), channel_id=1, source_target_pairs={{0,16},{4,20},{8,24},{12,28},{17,1},{21,5},{25,9},{29,13}} | collective-permute-start | bytes 884744 | tf_op jit(solution)/shard_map/ppermute | solution.py:752
  28.7 7.5 %copy-start.11 = (bf16[128,1024]{1,0:T(8,128)(2,1)}, bf16[128,1024]{1,0:T(8,128)(2,1)S(1)}, u32[]{:S(2)}) copy-start(bf16[128,1024]{1,0:T(8,128)(2,1)S(1)} %collective-permute-done.8.refs_0_.refs_14_.refs_5_) | copy-start | bytes 786436
  28.7 10.0 %collective-permute-start.4 = (bf16[144,1024]{1,0:T(8,128)(2,1)S(1)}, bf16[144,1024]{1,0:T(8,128)(2,1)S(1)}, u32[]{:S(2)}, u32[]{:S(2)}) collective-permute-start(bf16[144,1024]{1,0:T(8,128)(2,1)S(1)} %pair.2.refs_0_), channel_id=1, source_target_pairs={{0,8},{4,12},{16,24},{20,28},{9,1},{13,5},{25,17},{29,21}} | collective-permute-start | bytes 884744 | tf_op jit(solution)/shard_map/ppermute | solution.py:752
  36.2 6.0 %copy-start = (bf16[512,1024]{1,0:T(8,128)(2,1)S(1)}, bf16[512,1024]{1,0:T(8,128)(2,1)}, u32[]{:S(2)}) copy-start(bf16[512,1024]{1,0:T(8,128)(2,1)} %refs_0_.3) | copy-start | bytes 3145732
  36.2 0.7 copy-start.12
  38.7 2.1 %collective-permute-start.11 = (bf16[256,1024]{1,0:T(8,128)(2,1)}, bf16[256,1024]{1,0:T(8,128)(2,1)S(1)}, u32[]{:S(2)}, u32[]{:S(2)}) collective-permute-start(bf16[256,1024]{1,0:T(8,128)(2,1)} %stack.40), channel_id=1, source_target_pairs={{0,4},{4,0},{8,12},{12,8},{16,20},{20,16},{24,28},{28,24},{1,5},{5... | collective-permute-start | bytes 1572872 | tf_op jit(solution)/shard_map/ppermute | solution.py:617
  39.7 0.7 collective-permute-start.7
  40.8 0.8 copy-start.10
  40.8 1.3 copy-start.7
  48.2 8.2 %collective-permute-start.16 = (bf16[128,1024]{1,0:T(8,128)(2,1)S(1)}, bf16[128,1024]{1,0:T(8,128)(2,1)S(1)}, u32[]{:S(2)}, u32[]{:S(2)}) collective-permute-start(bf16[128,1024]{1,0:T(8,128)(2,1)S(1)} %get-tuple-element.106), channel_id=1, source_target_pairs={{0,1},{4,5},{8,9},{12,13},{16,17},{20,21},{24,25},{28,29}} | collective-permute-start | bytes 786440 | tf_op jit(solution)/shard_map/ppermute | solution.py:917
  48.9 8.9 %collective-permute-start.12 = (bf16[128,1024]{1,0:T(8,128)(2,1)S(1)}, bf16[128,1024]{1,0:T(8,128)(2,1)S(1)}, u32[]{:S(2)}, u32[]{:S(2)}) collective-permute-start(bf16[128,1024]{1,0:T(8,128)(2,1)S(1)} %get-tuple-element.102), channel_id=1, source_target_pairs={{0,1},{4,5},{8,9},{12,13},{16,17},{20,21},{24,25},{28,29}} | collective-permute-start | bytes 786440 | tf_op jit(solution)/shard_map/ppermute | solution.py:917
  56.5 22.7 %collective-permute-start.17 = (bf16[128,1024]{1,0:T(8,128)(2,1)S(1)}, bf16[128,1024]{1,0:T(8,128)(2,1)S(1)}, u32[]{:S(2)}, u32[]{:S(2)}) collective-permute-start(bf16[128,1024]{1,0:T(8,128)(2,1)S(1)} %add_convert_fusion.1.refs_12_), channel_id=1, source_target_pairs={{0,1},{1,2},{4,5},{5,6},{8,9},{9,10},{12,13},{13,14},{16,17},{17,1... | collective-permute-start | bytes 786440 | tf_op jit(solution)/shard_map/ppermute | solution.py:917
  57.9 27.5 %copy-start.3 = (bf16[128,1024]{1,0:T(8,128)(2,1)}, bf16[128,1024]{1,0:T(8,128)(2,1)S(1)}, u32[]{:S(2)}) copy-start(bf16[128,1024]{1,0:T(8,128)(2,1)S(1)} %add_convert_fusion.3.refs_13_) | copy-start | bytes 786436
  57.9 27.5 %collective-permute-start.13 = (bf16[128,1024]{1,0:T(8,128)(2,1)S(1)}, bf16[128,1024]{1,0:T(8,128)(2,1)S(1)}, u32[]{:S(2)}, u32[]{:S(2)}) collective-permute-start(bf16[128,1024]{1,0:T(8,128)(2,1)S(1)} %add_convert_fusion.3.refs_13_), channel_id=1, source_target_pairs={{0,1},{1,2},{4,5},{5,6},{8,9},{9,10},{12,13},{13,14},{16,17},{17,1... | collective-permute-start | bytes 786440 | tf_op jit(solution)/shard_map/ppermute | solution.py:917
  79.2 25.2 %copy-start.5 = (bf16[128,1024]{1,0:T(8,128)(2,1)}, bf16[128,1024]{1,0:T(8,128)(2,1)S(1)}, u32[]{:S(2)}) copy-start(bf16[128,1024]{1,0:T(8,128)(2,1)S(1)} %add_convert_fusion.refs_12_) | copy-start | bytes 786436
  79.2 11.8 %collective-permute-start.18 = (bf16[128,1024]{1,0:T(8,128)(2,1)S(1)}, bf16[128,1024]{1,0:T(8,128)(2,1)S(1)}, u32[]{:S(2)}, u32[]{:S(2)}) collective-permute-start(bf16[128,1024]{1,0:T(8,128)(2,1)S(1)} %add_convert_fusion.refs_12_), channel_id=1, source_target_pairs={{1,2},{2,3},{5,6},{6,7},{9,10},{10,11},{13,14},{14,15},{17,18},{18... | collective-permute-start | bytes 786440 | tf_op jit(solution)/shard_map/ppermute | solution.py:917
  85.4 13.3 %copy-start.1 = (bf16[128,1024]{1,0:T(8,128)(2,1)}, bf16[128,1024]{1,0:T(8,128)(2,1)S(1)}, u32[]{:S(2)}) copy-start(bf16[128,1024]{1,0:T(8,128)(2,1)S(1)} %add_convert_fusion.2.refs_0_.refs_13_) | copy-start | bytes 786436
  85.4 11.3 %collective-permute-start.14 = (bf16[128,1024]{1,0:T(8,128)(2,1)S(1)}, bf16[128,1024]{1,0:T(8,128)(2,1)S(1)}, u32[]{:S(2)}, u32[]{:S(2)}) collective-permute-start(bf16[128,1024]{1,0:T(8,128)(2,1)S(1)} %add_convert_fusion.2.refs_0_.refs_13_), channel_id=1, source_target_pairs={{1,2},{2,3},{5,6},{6,7},{9,10},{10,11},{13,14},{14,15},{17,18},{18... | collective-permute-start | bytes 786440 | tf_op jit(solution)/shard_map/ppermute | solution.py:917
  87.4 17.0 %collective-permute-start.15 = (bf16[128,1024]{1,0:T(8,128)(2,1)S(1)}, bf16[128,1024]{1,0:T(8,128)(2,1)S(1)}, u32[]{:S(2)}, u32[]{:S(2)}) collective-permute-start(bf16[128,1024]{1,0:T(8,128)(2,1)S(1)} %add_convert_fusion.2.refs_0_.refs_13_), channel_id=1, source_target_pairs={{1,3},{5,7},{9,11},{13,15},{17,19},{21,23},{25,27},{29,31}} | collective-permute-start | bytes 786440 | tf_op jit(solution)/shard_map/ppermute | solution.py:919
  91.0 13.4 %collective-permute-start.19 = (bf16[128,1024]{1,0:T(8,128)(2,1)S(1)}, bf16[128,1024]{1,0:T(8,128)(2,1)S(1)}, u32[]{:S(2)}, u32[]{:S(2)}) collective-permute-start(bf16[128,1024]{1,0:T(8,128)(2,1)S(1)} %collective-permute-done.18), channel_id=1, source_target_pairs={{2,3},{6,7},{10,11},{14,15},{18,19},{22,23},{26,27},{30,31}} | collective-permute-start | bytes 786440 | tf_op jit(solution)/shard_map/ppermute | solution.py:917
  96.8 7.6 %collective-permute-start.20 = (bf16[16,1024]{1,0:T(8,128)(2,1)S(1)}, bf16[16,1024]{1,0:T(8,128)(2,1)S(1)}, u32[]{:S(2)}, u32[]{:S(2)}) collective-permute-start(bf16[16,1024]{1,0:T(8,128)(2,1)S(1)} %slice_select_fusion), channel_id=1, source_target_pairs={{2,6},{6,10},{10,14},{14,18},{18,22},{22,26},{26,30},{7,3},{11,7},... | collective-permute-start | bytes 98312 | tf_op jit(solution)/shard_map/ppermute | solution.py:822
  111.9 5.2 %collective-permute-start.21 = (bf16[144,2048]{1,0:T(8,128)(2,1)S(1)}, bf16[144,2048]{1,0:T(8,128)(2,1)S(1)}, u32[]{:S(2)}, u32[]{:S(2)}) collective-permute-start(bf16[144,2048]{1,0:T(8,128)(2,1)S(1)} %get-tuple-element.120.mine), channel_id=1, source_target_pairs={{2,6},{6,2},{10,14},{14,10},{18,22},{22,18},{26,30},{30,26},{3,7},... | collective-permute-start | bytes 1769480 | tf_op jit(solution)/shard_map/ppermute | solution.py:743
  117.7 12.2 %collective-permute-start.24 = (bf16[144,1024]{1,0:T(8,128)(2,1)S(1)}, bf16[144,1024]{1,0:T(8,128)(2,1)S(1)}, u32[]{:S(2)}, u32[]{:S(2)}) collective-permute-start(bf16[144,1024]{1,0:T(8,128)(2,1)S(1)} %pair.3.refs_0_), channel_id=1, source_target_pairs={{2,26},{6,30},{10,18},{14,22},{19,11},{23,15},{27,3},{31,7}} | collective-permute-start | bytes 884744 | tf_op jit(solution)/shard_map/ppermute | solution.py:752
  119.0 17.1 %collective-permute-start.23 = (bf16[144,1024]{1,0:T(8,128)(2,1)S(1)}, bf16[144,1024]{1,0:T(8,128)(2,1)S(1)}, u32[]{:S(2)}, u32[]{:S(2)}) collective-permute-start(bf16[144,1024]{1,0:T(8,128)(2,1)S(1)} %pair.3.refs_0_), channel_id=1, source_target_pairs={{2,18},{6,22},{10,26},{14,30},{19,3},{23,7},{27,11},{31,15}} | collective-permute-start | bytes 884744 | tf_op jit(solution)/shard_map/ppermute | solution.py:752
  120.3 15.8 %collective-permute-start.22 = (bf16[144,1024]{1,0:T(8,128)(2,1)S(1)}, bf16[144,1024]{1,0:T(8,128)(2,1)S(1)}, u32[]{:S(2)}, u32[]{:S(2)}) collective-permute-start(bf16[144,1024]{1,0:T(8,128)(2,1)S(1)} %pair.3.refs_0_), channel_id=1, source_target_pairs={{2,10},{6,14},{18,26},{22,30},{11,3},{15,7},{27,19},{31,23}} | collective-permute-start | bytes 884744 | tf_op jit(solution)/shard_map/ppermute | solution.py:752
  122.8 17.8 %copy-start.4 = (bf16[128,1024]{1,0:T(8,128)(2,1)S(1)}, bf16[128,1024]{1,0:T(8,128)(2,1)}, u32[]{:S(2)}) copy-start(bf16[128,1024]{1,0:T(8,128)(2,1)} %copy-done.3) | copy-start | bytes 786436
  137.1 3.4 %collective-permute-start.25 = (bf16[128,1024]{1,0:T(8,128)(2,1)S(1)}, bf16[128,1024]{1,0:T(8,128)(2,1)S(1)}, u32[]{:S(2)}, u32[]{:S(2)}) collective-permute-start(bf16[128,1024]{1,0:T(8,128)(2,1)S(1)} %merge.3.refs_6_), channel_id=1, source_target_pairs={{2,6},{6,2},{10,14},{14,10},{18,22},{22,18},{26,30},{30,26},{3,7},... | collective-permute-start | bytes 786440 | tf_op jit(solution)/shard_map/ppermute | solution.py:743
  140.5 9.6 %copy-start.2 = (bf16[128,1024]{1,0:T(8,128)(2,1)S(1)}, bf16[128,1024]{1,0:T(8,128)(2,1)}, u32[]{:S(2)}) copy-start(bf16[128,1024]{1,0:T(8,128)(2,1)} %copy-done.1) | copy-start | bytes 786436
  140.5 9.6 %copy-start.6 = (bf16[128,1024]{1,0:T(8,128)(2,1)S(1)}, bf16[128,1024]{1,0:T(8,128)(2,1)}, u32[]{:S(2)}) copy-start(bf16[128,1024]{1,0:T(8,128)(2,1)} %copy-done.5) | copy-start | bytes 786436
  144.2 18.0 %collective-permute-start.28 = (bf16[128,1024]{1,0:T(8,128)(2,1)S(1)}, bf16[128,1024]{1,0:T(8,128)(2,1)S(1)}, u32[]{:S(2)}, u32[]{:S(2)}) collective-permute-start(bf16[128,1024]{1,0:T(8,128)(2,1)S(1)} %get-tuple-element.140.sent), channel_id=1, source_target_pairs={{2,3},{3,2},{1,0},{6,7},{7,6},{5,4},{10,11},{11,10},{9,8},{14,15},... | collective-permute-start | bytes 786440 | tf_op jit(solution)/shard_map/ppermute | solution.py:936
  146.2 14.7 %collective-permute-start.29 = (bf16[128,1024]{1,0:T(8,128)(2,1)S(1)}, bf16[128,1024]{1,0:T(8,128)(2,1)S(1)}, u32[]{:S(2)}, u32[]{:S(2)}) collective-permute-start(bf16[128,1024]{1,0:T(8,128)(2,1)S(1)} %get-tuple-element.142.sent), channel_id=1, source_target_pairs={{2,3},{3,2},{1,0},{6,7},{7,6},{5,4},{10,11},{11,10},{9,8},{14,15},... | collective-permute-start | bytes 786440 | tf_op jit(solution)/shard_map/ppermute | solution.py:936
  154.6 12.0 %collective-permute-start.27 = (bf16[128,1024]{1,0:T(8,128)(2,1)S(1)}, bf16[128,1024]{1,0:T(8,128)(2,1)S(1)}, u32[]{:S(2)}, u32[]{:S(2)}) collective-permute-start(bf16[128,1024]{1,0:T(8,128)(2,1)S(1)} %get-tuple-element.138.sent), channel_id=1, source_target_pairs={{2,3},{3,2},{1,0},{6,7},{7,6},{5,4},{10,11},{11,10},{9,8},{14,15},... | collective-permute-start | bytes 786440 | tf_op jit(solution)/shard_map/ppermute | solution.py:936
  156.5 14.8 %collective-permute-start.26 = (bf16[128,1024]{1,0:T(8,128)(2,1)S(1)}, bf16[128,1024]{1,0:T(8,128)(2,1)S(1)}, u32[]{:S(2)}, u32[]{:S(2)}) collective-permute-start(bf16[128,1024]{1,0:T(8,128)(2,1)S(1)} %get-tuple-element.136.sent), channel_id=1, source_target_pairs={{2,3},{3,2},{1,0},{6,7},{7,6},{5,4},{10,11},{11,10},{9,8},{14,15},... | collective-permute-start | bytes 786440 | tf_op jit(solution)/shard_map/ppermute | solution.py:936

commit v2 on v1

--- a/solution.py
+++ b/solution.py
@@ -484,6 +484,8 @@
     resident = not isinstance(pieces, list)
     place = near_one if resident else far
     spread, gain = place(params[5]), place(params[7])
+    if resident:
+        mine, other, partner = near(mine, other, partner)
     plan = [] if resident else [ranges for _, ranges in pieces]
     shard_rows = inner // lax.axis_size("seq")
     count = len(members)

time: 173 us -> 173 us (level)
  no operation moved by 1% of the time
where the time goes in v2:
time: 173 us
  Pallas kernels  70.4 us (41%)
  waiting for transfers between devices  55 us (32%)
  starting transfers between devices  43.2 us (25%)
  local copies, waits for them, and re-layouts  2.14 us (1%)
    ppermute x7, waiting for transfers between devices, per_device(): received.append(lax.ppermute(value, 'section', pairs))  31.5 us
    pallas_call x4, Pallas kernels, finish(): pl.pallas_call(functools.partial(finish_kernel, plan, shard_rows, members...  20.7 us
    pallas_call x2, Pallas kernels, prep(): pl.pallas_call(prep_kernel, grid_spec=grid_spec, out_shape=[kept((length,...  18.3 us
    pallas_call x2, Pallas kernels, mid(): pl.pallas_call(mid_kernel, grid=(steps,), in_specs=[whole_block((length,...  12.7 us
    ppermute x4, starting transfers between devices, per_device(): lax.ppermute(terms[index], 'section', [(low, high), (high, low), (1, 0)])  11.7 us
    ppermute x7, starting transfers between devices, per_device(): received.append(lax.ppermute(value, 'section', pairs))  9.25 us
    ppermute x6, waiting for transfers between devices, forward(): return lax.ppermute(value, ('seq', 'section'), pairs)  7.42 us
    ppermute x6, starting transfers between devices, forward(): return lax.ppermute(value, ('seq', 'section'), pairs)  7.02 us
  transfers between devices with their start and end apart: 30, of which 15 were waited for; matrix products, arithmetic and copies ran while one was open for 0% of the time, Pallas kernels for 27%

profile of v2, /device:TPU:20, one launch (start us, length us, event | category | flops | bytes accessed | tf_op | source)
XLA Modules:
  0.0 172.6 jit_solution(15506442672379534069)
XLA Ops:
  2.0 1.5 collective-permute-start.1
  3.6 10.9 %prep.2 = (bf16[512,1024]{1,0:T(8,128)(2,1)S(1)}, bf16[512,2048]{1,0:T(8,128)(2,1)S(1)}, bf16[512,128]{1,0:T(8,128)(2,1)S(1)}, bf16[512,128]{1,0:T(8,128)(2,1)S(...) custom-call(s32[7]{0:T(128)S(1)} %stack.37.info, ...), custom_call_target="tpu_custom_call" | custom-call | flops 2147483648 | bytes 12582912 | tf_op jit(solution)/shard_map/prep/pallas_call | solution.py:411
  14.6 0.8 collective-permute-done.2.refs_0_.refs_4_.refs_13_
  17.0 2.7 %stack.39 = (bf16[128,1024]{1,0:T(8,128)(2,1)}, bf16[128,1024]{1,0:T(8,128)(2,1)}, bf16[768,1024]{1,0:T(8,128)(2,1)}) custom-call(bf16[256,1024]{1,0:T(8,128)(2,1)} %copy-done.8, bf16[256,1024]{1,0:T(8,128)(2,1)} %copy-done.9, bf16[256,1024]{1,0:T(8,128)(2,1)} %bitcast.11, bf16[256,1024]{1,0:T(8,128)(2,1)} %copy-done.9, bf16[256,1024]{1,0:T(8,128)(2,1)} %copy-done.8), custom_call_target="tpu_custom_call" | custom-call | flops 1000000 | bytes 1000000 | tf_op jit(solution)/shard_map/stack/pallas_call | solution.py:603
  19.8 1.6 collective-permute-start.8
  21.3 1.5 collective-permute-start.9
  24.2 4.5 %collective-permute-done.8.refs_0_.refs_14_.refs_5_ = bf16[128,1024]{1,0:T(8,128)(2,1)S(1)} collective-permute-done((bf16[128,1024]{1,0:T(8,128)(2,1)}, bf16[128,1024]{1,0:T(8,128)(2,1)S(1)}, u32[]{:S(2)}, u32[]{:S(2)}) %collective-permute-start.8) | collective-permute-done | bytes 262176 | tf_op jit(solution)/shard_map/ppermute | solution.py:619
  29.4 6.8 %mid.2 = (f32[512,2048]{1,0:T(8,128)S(1)}, bf16[512,2048]{1,0:T(8,128)(2,1)S(1)}) custom-call(bf16[512,1024]{1,0:T(8,128)(2,1)S(1)} %get-tuple-element.79.normed, bf16[1,1024,4096]{2,1,0:T(8,128)(2,1)} %refs_1_.1, bf16[512,2048]{1,0:T(8,128)(2,1)S(1)} %get-tuple-element.80.x, bf16[512,128]{1,0:T(8,128)(2,1)S(1)} %get-tuple-element.81.b, ...), custom_call_target="tpu_custom_call" | custom-call | flops 2147483648 | bytes 12582912 | tf_op jit(solution)/shard_map/mid/pallas_call | solution.py:443
  36.9 1.8 %stack.40 = bf16[256,1024]{1,0:T(8,128)(2,1)} custom-call(bf16[128,1024]{1,0:T(8,128)(2,1)} %copy-done.11, bf16[128,1024]{1,0:T(8,128)(2,1)} %copy-done.12), custom_call_target="tpu_custom_call" | custom-call | flops 1000000 | bytes 1000000 | tf_op jit(solution)/shard_map/stack/pallas_call | solution.py:603
  38.7 0.9 merge.2.refs_6_
  42.2 6.0 %finish.5 = (bf16[128,1024]{1,0:T(8,128)(2,1)S(1)}, bf16[128,1024]{1,0:T(8,128)(2,1)S(1)}, f32[128,1024]{1,0:T(8,128)S(1)}, f32[128,1024]{1,0:T(8,128)S(1)}) custom-call(s32[7]{0:T(128)S(1)} %stack.37.info, bf16[512,1024]{1,0:T(8,128)(2,1)S(1)} %copy-done, f32[512,2048]{1,0:T(8,128)S(1)} %get-tuple-element.85.refs_1_, ...), custom_call_target="tpu_custom_call" | custom-call | flops 1073741824 | bytes 8388608 | tf_op jit(solution)/shard_map/finish/pallas_call | solution.py:506
  48.9 0.9 collective-permute-start.12
  49.7 6.6 %finish.4 = (bf16[128,1024]{1,0:T(8,128)(2,1)S(1)}, bf16[128,1024]{1,0:T(8,128)(2,1)S(1)}, f32[128,1024]{1,0:T(8,128)S(1)}, f32[128,1024]{1,0:T(8,128)S(1)}) custom-call(s32[7]{0:T(128)S(1)} %stack.37.info, bf16[512,1024]{1,0:T(8,128)(2,1)S(1)} %copy-done, f32[512,2048]{1,0:T(8,128)S(1)} %get-tuple-element.85.refs_1_, ...), custom_call_target="tpu_custom_call" | custom-call | flops 1073741824 | bytes 8388608 | tf_op jit(solution)/shard_map/finish/pallas_call | solution.py:506
  56.5 1.3 collective-permute-start.17
  57.9 1.3 collective-permute-start.13
  59.2 19.9 %collective-permute-done.17 = bf16[128,1024]{1,0:T(8,128)(2,1)S(1)} collective-permute-done((bf16[128,1024]{1,0:T(8,128)(2,1)S(1)}, bf16[128,1024]{1,0:T(8,128)(2,1)S(1)}, u32[]{:S(2)}, u32[]{:S(2)}) %collective-permute-start.17) | collective-permute-done | bytes 262176 | tf_op jit(solution)/shard_map/ppermute | solution.py:919
  79.2 1.9 %collective-permute-start.18 = (bf16[128,1024]{1,0:T(8,128)(2,1)S(1)}, bf16[128,1024]{1,0:T(8,128)(2,1)S(1)}, u32[]{:S(2)}, u32[]{:S(2)}) collective-permute-start(bf16[128,1024]{1,0:T(8,128)(2,1)S(1)} %add_convert_fusion.refs_12_), channel_id=1, source_target_pairs={{1,2},{2,3},{5,6},{6,7},{9,10},{10,11},{13,14},{14,15},{17,18},{18... | collective-permute-start | bytes 786440 | tf_op jit(solution)/shard_map/ppermute | solution.py:919
  81.1 4.2 %collective-permute-done.13 = bf16[128,1024]{1,0:T(8,128)(2,1)S(1)} collective-permute-done((bf16[128,1024]{1,0:T(8,128)(2,1)S(1)}, bf16[128,1024]{1,0:T(8,128)(2,1)S(1)}, u32[]{:S(2)}, u32[]{:S(2)}) %collective-permute-start.13) | collective-permute-done | bytes 262176 | tf_op jit(solution)/shard_map/ppermute | solution.py:919
  85.4 1.9 %collective-permute-start.14 = (bf16[128,1024]{1,0:T(8,128)(2,1)S(1)}, bf16[128,1024]{1,0:T(8,128)(2,1)S(1)}, u32[]{:S(2)}, u32[]{:S(2)}) collective-permute-start(bf16[128,1024]{1,0:T(8,128)(2,1)S(1)} %add_convert_fusion.2.refs_0_.refs_13_), channel_id=1, source_target_pairs={{1,2},{2,3},{5,6},{6,7},{9,10},{10,11},{13,14},{14,15},{17,18},{18... | collective-permute-start | bytes 786440 | tf_op jit(solution)/shard_map/ppermute | solution.py:919
  88.0 2.9 %collective-permute-done.18 = bf16[128,1024]{1,0:T(8,128)(2,1)S(1)} collective-permute-done((bf16[128,1024]{1,0:T(8,128)(2,1)S(1)}, bf16[128,1024]{1,0:T(8,128)(2,1)S(1)}, u32[]{:S(2)}, u32[]{:S(2)}) %collective-permute-start.18) | collective-permute-done | bytes 262176 | tf_op jit(solution)/shard_map/ppermute | solution.py:919
  91.0 1.3 collective-permute-start.19
  92.3 4.5 %collective-permute-done.14 = bf16[128,1024]{1,0:T(8,128)(2,1)S(1)} collective-permute-done((bf16[128,1024]{1,0:T(8,128)(2,1)S(1)}, bf16[128,1024]{1,0:T(8,128)(2,1)S(1)}, u32[]{:S(2)}, u32[]{:S(2)}) %collective-permute-start.14) | collective-permute-done | bytes 262176 | tf_op jit(solution)/shard_map/ppermute | solution.py:919
  96.8 1.9 %collective-permute-start.20 = (bf16[16,1024]{1,0:T(8,128)(2,1)S(1)}, bf16[16,1024]{1,0:T(8,128)(2,1)S(1)}, u32[]{:S(2)}, u32[]{:S(2)}) collective-permute-start(bf16[16,1024]{1,0:T(8,128)(2,1)S(1)} %slice_select_fusion), channel_id=1, source_target_pairs={{2,6},{6,10},{10,14},{14,18},{18,22},{22,26},{26,30},{7,3},{11,7},... | collective-permute-start | bytes 98312 | tf_op jit(solution)/shard_map/ppermute | solution.py:824
  98.7 5.6 %hold.1 = (bf16[1,1024,4096]{2,1,0:T(8,128)(2,1)S(1)}, bf16[2048,1024]{1,0:T(8,128)(2,1)S(1)}, f32[1,1024]{1,0:T(1,128)S(1)}, bf16[1,288,1024]{2,1,0:T(8,128)(2,...) custom-call(s32[7]{0:T(128)S(1)} %stack.37.info, ...), custom_call_target="tpu_custom_call" | custom-call | flops 1000000 | bytes 25165824 | tf_op jit(solution)/shard_map/hold/pallas_call | solution.py:550
  104.5 7.3 %prep.3 = (bf16[512,1024]{1,0:T(8,128)(2,1)S(1)}, bf16[512,2048]{1,0:T(8,128)(2,1)S(1)}, bf16[512,128]{1,0:T(8,128)(2,1)S(1)}, bf16[512,128]{1,0:T(8,128)(2,1)S(...) custom-call(s32[7]{0:T(128)S(1)} %stack.37.info, ...), custom_call_target="tpu_custom_call" | custom-call | flops 2147483648 | bytes 12582912 | tf_op jit(solution)/shard_map/prep/pallas_call | solution.py:411
  111.9 3.6 %collective-permute-start.21 = (bf16[144,2048]{1,0:T(8,128)(2,1)S(1)}, bf16[144,2048]{1,0:T(8,128)(2,1)S(1)}, u32[]{:S(2)}, u32[]{:S(2)}) collective-permute-start(bf16[144,2048]{1,0:T(8,128)(2,1)S(1)} %get-tuple-element.120.mine), channel_id=1, source_target_pairs={{2,6},{6,2},{10,14},{14,10},{18,22},{22,18},{26,30},{30,26},{3,7},... | collective-permute-start | bytes 1769480 | tf_op jit(solution)/shard_map/ppermute | solution.py:745
  115.4 1.6 collective-permute-done.21.partner.refs_8_
  117.7 1.3 collective-permute-start.24
  119.0 1.3 collective-permute-start.23
  120.3 2.4 %collective-permute-start.22 = (bf16[144,1024]{1,0:T(8,128)(2,1)S(1)}, bf16[144,1024]{1,0:T(8,128)(2,1)S(1)}, u32[]{:S(2)}, u32[]{:S(2)}) collective-permute-start(bf16[144,1024]{1,0:T(8,128)(2,1)S(1)} %pair.3.refs_0_), channel_id=1, source_target_pairs={{2,10},{6,14},{18,26},{22,30},{11,3},{15,7},{27,19},{31,23}} | collective-permute-start | bytes 884744 | tf_op jit(solution)/shard_map/ppermute | solution.py:754
  122.8 5.9 %mid.3 = (f32[512,2048]{1,0:T(8,128)S(1)}, bf16[512,2048]{1,0:T(8,128)(2,1)S(1)}) custom-call(bf16[512,1024]{1,0:T(8,128)(2,1)S(1)} %get-tuple-element.121.normed, bf16[1,1024,4096]{2,1,0:T(8,128)(2,1)S(1)} %get-tuple-element.113.wide.gate_weight, bf16[512,2048]{1,0:T(8,128)(2,1)S(1)} %get-tuple-element.122.x, bf16[512,128]{1,0:T(8,128)(2,1)S(1)} %get-tuple-element.123.b, ...), custom_call_target="tpu_custom_call" | custom-call | flops 2147483648 | bytes 12582912 | tf_op jit(solution)/shard_map/mid/pallas_call | solution.py:443
  128.7 1.2 collective-permute-done.24.refs_3_
  129.9 6.2 %collective-permute-done.23.refs_2_ = bf16[144,1024]{1,0:T(8,128)(2,1)S(1)} collective-permute-done((bf16[144,1024]{1,0:T(8,128)(2,1)S(1)}, bf16[144,1024]{1,0:T(8,128)(2,1)S(1)}, u32[]{:S(2)}, u32[]{:S(2)}) %collective-permute-start.23) | collective-permute-done | bytes 294944 | tf_op jit(solution)/shard_map/ppermute | solution.py:754
  136.1 0.9 merge.3.refs_6_
  137.1 2.0 %collective-permute-start.25 = (bf16[128,1024]{1,0:T(8,128)(2,1)S(1)}, bf16[128,1024]{1,0:T(8,128)(2,1)S(1)}, u32[]{:S(2)}, u32[]{:S(2)}) collective-permute-start(bf16[128,1024]{1,0:T(8,128)(2,1)S(1)} %merge.3.refs_6_), channel_id=1, source_target_pairs={{2,6},{6,2},{10,14},{14,10},{18,22},{22,18},{26,30},{30,26},{3,7},... | collective-permute-start | bytes 786440 | tf_op jit(solution)/shard_map/ppermute | solution.py:745
  139.1 1.5 collective-permute-done.25.refs_7_
  140.5 3.7 %finish.7 = (bf16[128,1024]{1,0:T(8,128)(2,1)S(1)}, bf16[128,1024]{1,0:T(8,128)(2,1)S(1)}, f32[128,1024]{1,0:T(8,128)S(1)}, f32[128,1024]{1,0:T(8,128)S(1)}) custom-call(s32[7]{0:T(128)S(1)} %stack.37.info, bf16[512,1024]{1,0:T(8,128)(2,1)S(1)} %pad_maximum_fusion.rows.refs_0_, f32[512,2048]{1,0:T(8,128)S(1)} %get-tuple-element.128.refs_1_, ...), custom_call_target="tpu_custom_call" | custom-call | flops 1073741824 | bytes 8388608 | tf_op jit(solution)/shard_map/finish/pallas_call | solution.py:506
  144.2 2.0 %collective-permute-start.28 = (bf16[128,1024]{1,0:T(8,128)(2,1)S(1)}, bf16[128,1024]{1,0:T(8,128)(2,1)S(1)}, u32[]{:S(2)}, u32[]{:S(2)}) collective-permute-start(bf16[128,1024]{1,0:T(8,128)(2,1)S(1)} %get-tuple-element.140.sent), channel_id=1, source_target_pairs={{2,3},{3,2},{1,0},{6,7},{7,6},{5,4},{10,11},{11,10},{9,8},{14,15},... | collective-permute-start | bytes 786440 | tf_op jit(solution)/shard_map/ppermute | solution.py:938
  146.2 3.9 %collective-permute-start.29 = (bf16[128,1024]{1,0:T(8,128)(2,1)S(1)}, bf16[128,1024]{1,0:T(8,128)(2,1)S(1)}, u32[]{:S(2)}, u32[]{:S(2)}) collective-permute-start(bf16[128,1024]{1,0:T(8,128)(2,1)S(1)} %get-tuple-element.142.sent), channel_id=1, source_target_pairs={{2,3},{3,2},{1,0},{6,7},{7,6},{5,4},{10,11},{11,10},{9,8},{14,15},... | collective-permute-start | bytes 786440 | tf_op jit(solution)/shard_map/ppermute | solution.py:938
  150.1 4.4 %finish.6 = (bf16[128,1024]{1,0:T(8,128)(2,1)S(1)}, bf16[128,1024]{1,0:T(8,128)(2,1)S(1)}, f32[128,1024]{1,0:T(8,128)S(1)}, f32[128,1024]{1,0:T(8,128)S(1)}) custom-call(s32[7]{0:T(128)S(1)} %stack.37.info, bf16[512,1024]{1,0:T(8,128)(2,1)S(1)} %pad_maximum_fusion.rows.refs_0_, f32[512,2048]{1,0:T(8,128)S(1)} %get-tuple-element.128.refs_1_, ...), custom_call_target="tpu_custom_call" | custom-call | flops 1073741824 | bytes 8388608 | tf_op jit(solution)/shard_map/finish/pallas_call | solution.py:506
  154.6 2.0 %collective-permute-start.27 = (bf16[128,1024]{1,0:T(8,128)(2,1)S(1)}, bf16[128,1024]{1,0:T(8,128)(2,1)S(1)}, u32[]{:S(2)}, u32[]{:S(2)}) collective-permute-start(bf16[128,1024]{1,0:T(8,128)(2,1)S(1)} %get-tuple-element.138.sent), channel_id=1, source_target_pairs={{2,3},{3,2},{1,0},{6,7},{7,6},{5,4},{10,11},{11,10},{9,8},{14,15},... | collective-permute-start | bytes 786440 | tf_op jit(solution)/shard_map/ppermute | solution.py:938
  156.5 3.9 %collective-permute-start.26 = (bf16[128,1024]{1,0:T(8,128)(2,1)S(1)}, bf16[128,1024]{1,0:T(8,128)(2,1)S(1)}, u32[]{:S(2)}, u32[]{:S(2)}) collective-permute-start(bf16[128,1024]{1,0:T(8,128)(2,1)S(1)} %get-tuple-element.136.sent), channel_id=1, source_target_pairs={{2,3},{3,2},{1,0},{6,7},{7,6},{5,4},{10,11},{11,10},{9,8},{14,15},... | collective-permute-start | bytes 786440 | tf_op jit(solution)/shard_map/ppermute | solution.py:938
  160.9 1.3 settle.4.rest_0_
  162.2 1.3 settle.5.rest_0_
  163.5 3.0 %collective-permute-done.27.other = bf16[128,1024]{1,0:T(8,128)(2,1)S(1)} collective-permute-done((bf16[128,1024]{1,0:T(8,128)(2,1)S(1)}, bf16[128,1024]{1,0:T(8,128)(2,1)S(1)}, u32[]{:S(2)}, u32[]{:S(2)}) %collective-permute-start.27) | collective-permute-done | bytes 262176 | tf_op jit(solution)/shard_map/ppermute | solution.py:938
  166.5 1.3 settle.6.rest_0_
  167.8 3.5 %collective-permute-done.26.other = bf16[128,1024]{1,0:T(8,128)(2,1)S(1)} collective-permute-done((bf16[128,1024]{1,0:T(8,128)(2,1)S(1)}, bf16[128,1024]{1,0:T(8,128)(2,1)S(1)}, u32[]{:S(2)}, u32[]{:S(2)}) %collective-permute-start.26) | collective-permute-done | bytes 262176 | tf_op jit(solution)/shard_map/ppermute | solution.py:938
  171.3 1.3 settle.7
  (68 shorter events, 12.0 us)
Async XLA Ops:
  0.8 0.7 collective-permute-start
  1.5 13.9 %collective-permute-start.2 = (bf16[256,1024]{1,0:T(8,128)(2,1)}, bf16[256,1024]{1,0:T(8,128)(2,1)S(1)}, u32[]{:S(2)}, u32[]{:S(2)}) collective-permute-start(bf16[256,1024]{1,0:T(8,128)(2,1)} %bitcast.9), channel_id=1, source_target_pairs={{0,16},{4,20},{8,24},{12,28},{16,0},{20,4},{24,8},{28,12},{1,17},{... | collective-permute-start | bytes 1572872 | tf_op jit(solution)/shard_map/ppermute | solution.py:619
  2.0 13.6 %collective-permute-start.1 = (bf16[256,1024]{1,0:T(8,128)(2,1)}, bf16[256,1024]{1,0:T(8,128)(2,1)S(1)}, u32[]{:S(2)}, u32[]{:S(2)}) collective-permute-start(bf16[256,1024]{1,0:T(8,128)(2,1)} %bitcast.10), channel_id=1, source_target_pairs={{0,8},{4,12},{8,0},{12,4},{16,24},{20,28},{24,16},{28,20},{1,9},{5... | collective-permute-start | bytes 1572872 | tf_op jit(solution)/shard_map/ppermute | solution.py:619
  15.4 1.6 copy-start.8
  15.6 1.4 copy-start.9
  15.6 0.7 collective-permute-start.3
  19.8 21.1 %collective-permute-start.10 = (bf16[768,1024]{1,0:T(8,128)(2,1)}, bf16[768,1024]{1,0:T(8,128)(2,1)S(1)}, u32[]{:S(2)}, u32[]{:S(2)}) collective-permute-start(bf16[768,1024]{1,0:T(8,128)(2,1)} %get-tuple-element.99), channel_id=1, source_target_pairs={{0,4},{4,0},{8,12},{12,8},{16,20},{20,16},{24,28},{28,24},{1,5},{5... | collective-permute-start | bytes 4718600 | tf_op jit(solution)/shard_map/ppermute | solution.py:619
  19.8 8.9 %collective-permute-start.8 = (bf16[128,1024]{1,0:T(8,128)(2,1)}, bf16[128,1024]{1,0:T(8,128)(2,1)S(1)}, u32[]{:S(2)}, u32[]{:S(2)}) collective-permute-start(bf16[128,1024]{1,0:T(8,128)(2,1)} %get-tuple-element.95), channel_id=1, source_target_pairs={{0,8},{4,12},{8,0},{12,4},{16,24},{20,28},{24,16},{28,20},{1,9},{5... | collective-permute-start | bytes 786440 | tf_op jit(solution)/shard_map/ppermute | solution.py:619
  21.3 14.9 %collective-permute-start.9 = (bf16[128,1024]{1,0:T(8,128)(2,1)}, bf16[128,1024]{1,0:T(8,128)(2,1)S(1)}, u32[]{:S(2)}, u32[]{:S(2)}) collective-permute-start(bf16[128,1024]{1,0:T(8,128)(2,1)} %get-tuple-element.96), channel_id=1, source_target_pairs={{0,16},{4,20},{8,24},{12,28},{16,0},{20,4},{24,8},{28,12},{1,17},{... | collective-permute-start | bytes 786440 | tf_op jit(solution)/shard_map/ppermute | solution.py:619
  22.8 15.9 %collective-permute-start.6 = (bf16[144,1024]{1,0:T(8,128)(2,1)S(1)}, bf16[144,1024]{1,0:T(8,128)(2,1)S(1)}, u32[]{:S(2)}, u32[]{:S(2)}) collective-permute-start(bf16[144,1024]{1,0:T(8,128)(2,1)S(1)} %pair.2.refs_0_), channel_id=1, source_target_pairs={{0,24},{4,28},{8,16},{12,20},{17,9},{21,13},{25,1},{29,5}} | collective-permute-start | bytes 884744 | tf_op jit(solution)/shard_map/ppermute | solution.py:754
  23.5 15.2 %collective-permute-start.5 = (bf16[144,1024]{1,0:T(8,128)(2,1)S(1)}, bf16[144,1024]{1,0:T(8,128)(2,1)S(1)}, u32[]{:S(2)}, u32[]{:S(2)}) collective-permute-start(bf16[144,1024]{1,0:T(8,128)(2,1)S(1)} %pair.2.refs_0_), channel_id=1, source_target_pairs={{0,16},{4,20},{8,24},{12,28},{17,1},{21,5},{25,9},{29,13}} | collective-permute-start | bytes 884744 | tf_op jit(solution)/shard_map/ppermute | solution.py:754
  28.7 7.5 %copy-start.11 = (bf16[128,1024]{1,0:T(8,128)(2,1)}, bf16[128,1024]{1,0:T(8,128)(2,1)S(1)}, u32[]{:S(2)}) copy-start(bf16[128,1024]{1,0:T(8,128)(2,1)S(1)} %collective-permute-done.8.refs_0_.refs_14_.refs_5_) | copy-start | bytes 786436
  28.7 10.0 %collective-permute-start.4 = (bf16[144,1024]{1,0:T(8,128)(2,1)S(1)}, bf16[144,1024]{1,0:T(8,128)(2,1)S(1)}, u32[]{:S(2)}, u32[]{:S(2)}) collective-permute-start(bf16[144,1024]{1,0:T(8,128)(2,1)S(1)} %pair.2.refs_0_), channel_id=1, source_target_pairs={{0,8},{4,12},{16,24},{20,28},{9,1},{13,5},{25,17},{29,21}} | collective-permute-start | bytes 884744 | tf_op jit(solution)/shard_map/ppermute | solution.py:754
  36.2 6.0 %copy-start = (bf16[512,1024]{1,0:T(8,128)(2,1)S(1)}, bf16[512,1024]{1,0:T(8,128)(2,1)}, u32[]{:S(2)}) copy-start(bf16[512,1024]{1,0:T(8,128)(2,1)} %refs_0_.3) | copy-start | bytes 3145732
  36.2 0.7 copy-start.12
  38.7 2.1 %collective-permute-start.11 = (bf16[256,1024]{1,0:T(8,128)(2,1)}, bf16[256,1024]{1,0:T(8,128)(2,1)S(1)}, u32[]{:S(2)}, u32[]{:S(2)}) collective-permute-start(bf16[256,1024]{1,0:T(8,128)(2,1)} %stack.40), channel_id=1, source_target_pairs={{0,4},{4,0},{8,12},{12,8},{16,20},{20,16},{24,28},{28,24},{1,5},{5... | collective-permute-start | bytes 1572872 | tf_op jit(solution)/shard_map/ppermute | solution.py:619
  39.7 0.7 collective-permute-start.7
  40.8 0.8 copy-start.10
  40.8 1.3 copy-start.7
  48.2 8.2 %collective-permute-start.16 = (bf16[128,1024]{1,0:T(8,128)(2,1)S(1)}, bf16[128,1024]{1,0:T(8,128)(2,1)S(1)}, u32[]{:S(2)}, u32[]{:S(2)}) collective-permute-start(bf16[128,1024]{1,0:T(8,128)(2,1)S(1)} %get-tuple-element.106), channel_id=1, source_target_pairs={{0,1},{4,5},{8,9},{12,13},{16,17},{20,21},{24,25},{28,29}} | collective-permute-start | bytes 786440 | tf_op jit(solution)/shard_map/ppermute | solution.py:919
  48.9 8.9 %collective-permute-start.12 = (bf16[128,1024]{1,0:T(8,128)(2,1)S(1)}, bf16[128,1024]{1,0:T(8,128)(2,1)S(1)}, u32[]{:S(2)}, u32[]{:S(2)}) collective-permute-start(bf16[128,1024]{1,0:T(8,128)(2,1)S(1)} %get-tuple-element.102), channel_id=1, source_target_pairs={{0,1},{4,5},{8,9},{12,13},{16,17},{20,21},{24,25},{28,29}} | collective-permute-start | bytes 786440 | tf_op jit(solution)/shard_map/ppermute | solution.py:919
  56.5 22.7 %collective-permute-start.17 = (bf16[128,1024]{1,0:T(8,128)(2,1)S(1)}, bf16[128,1024]{1,0:T(8,128)(2,1)S(1)}, u32[]{:S(2)}, u32[]{:S(2)}) collective-permute-start(bf16[128,1024]{1,0:T(8,128)(2,1)S(1)} %add_convert_fusion.1.refs_12_), channel_id=1, source_target_pairs={{0,1},{1,2},{4,5},{5,6},{8,9},{9,10},{12,13},{13,14},{16,17},{17,1... | collective-permute-start | bytes 786440 | tf_op jit(solution)/shard_map/ppermute | solution.py:919
  57.9 27.5 %copy-start.3 = (bf16[128,1024]{1,0:T(8,128)(2,1)}, bf16[128,1024]{1,0:T(8,128)(2,1)S(1)}, u32[]{:S(2)}) copy-start(bf16[128,1024]{1,0:T(8,128)(2,1)S(1)} %add_convert_fusion.3.refs_13_) | copy-start | bytes 786436
  57.9 27.5 %collective-permute-start.13 = (bf16[128,1024]{1,0:T(8,128)(2,1)S(1)}, bf16[128,1024]{1,0:T(8,128)(2,1)S(1)}, u32[]{:S(2)}, u32[]{:S(2)}) collective-permute-start(bf16[128,1024]{1,0:T(8,128)(2,1)S(1)} %add_convert_fusion.3.refs_13_), channel_id=1, source_target_pairs={{0,1},{1,2},{4,5},{5,6},{8,9},{9,10},{12,13},{13,14},{16,17},{17,1... | collective-permute-start | bytes 786440 | tf_op jit(solution)/shard_map/ppermute | solution.py:919
  79.2 25.2 %copy-start.5 = (bf16[128,1024]{1,0:T(8,128)(2,1)}, bf16[128,1024]{1,0:T(8,128)(2,1)S(1)}, u32[]{:S(2)}) copy-start(bf16[128,1024]{1,0:T(8,128)(2,1)S(1)} %add_convert_fusion.refs_12_) | copy-start | bytes 786436
  79.2 11.8 %collective-permute-start.18 = (bf16[128,1024]{1,0:T(8,128)(2,1)S(1)}, bf16[128,1024]{1,0:T(8,128)(2,1)S(1)}, u32[]{:S(2)}, u32[]{:S(2)}) collective-permute-start(bf16[128,1024]{1,0:T(8,128)(2,1)S(1)} %add_convert_fusion.refs_12_), channel_id=1, source_target_pairs={{1,2},{2,3},{5,6},{6,7},{9,10},{10,11},{13,14},{14,15},{17,18},{18... | collective-permute-start | bytes 786440 | tf_op jit(solution)/shard_map/ppermute | solution.py:919
  85.4 13.3 %copy-start.1 = (bf16[128,1024]{1,0:T(8,128)(2,1)}, bf16[128,1024]{1,0:T(8,128)(2,1)S(1)}, u32[]{:S(2)}) copy-start(bf16[128,1024]{1,0:T(8,128)(2,1)S(1)} %add_convert_fusion.2.refs_0_.refs_13_) | copy-start | bytes 786436
  85.4 11.3 %collective-permute-start.14 = (bf16[128,1024]{1,0:T(8,128)(2,1)S(1)}, bf16[128,1024]{1,0:T(8,128)(2,1)S(1)}, u32[]{:S(2)}, u32[]{:S(2)}) collective-permute-start(bf16[128,1024]{1,0:T(8,128)(2,1)S(1)} %add_convert_fusion.2.refs_0_.refs_13_), channel_id=1, source_target_pairs={{1,2},{2,3},{5,6},{6,7},{9,10},{10,11},{13,14},{14,15},{17,18},{18... | collective-permute-start | bytes 786440 | tf_op jit(solution)/shard_map/ppermute | solution.py:919
  87.4 17.0 %collective-permute-start.15 = (bf16[128,1024]{1,0:T(8,128)(2,1)S(1)}, bf16[128,1024]{1,0:T(8,128)(2,1)S(1)}, u32[]{:S(2)}, u32[]{:S(2)}) collective-permute-start(bf16[128,1024]{1,0:T(8,128)(2,1)S(1)} %add_convert_fusion.2.refs_0_.refs_13_), channel_id=1, source_target_pairs={{1,3},{5,7},{9,11},{13,15},{17,19},{21,23},{25,27},{29,31}} | collective-permute-start | bytes 786440 | tf_op jit(solution)/shard_map/ppermute | solution.py:921
  91.0 13.4 %collective-permute-start.19 = (bf16[128,1024]{1,0:T(8,128)(2,1)S(1)}, bf16[128,1024]{1,0:T(8,128)(2,1)S(1)}, u32[]{:S(2)}, u32[]{:S(2)}) collective-permute-start(bf16[128,1024]{1,0:T(8,128)(2,1)S(1)} %collective-permute-done.18), channel_id=1, source_target_pairs={{2,3},{6,7},{10,11},{14,15},{18,19},{22,23},{26,27},{30,31}} | collective-permute-start | bytes 786440 | tf_op jit(solution)/shard_map/ppermute | solution.py:919
  96.8 7.6 %collective-permute-start.20 = (bf16[16,1024]{1,0:T(8,128)(2,1)S(1)}, bf16[16,1024]{1,0:T(8,128)(2,1)S(1)}, u32[]{:S(2)}, u32[]{:S(2)}) collective-permute-start(bf16[16,1024]{1,0:T(8,128)(2,1)S(1)} %slice_select_fusion), channel_id=1, source_target_pairs={{2,6},{6,10},{10,14},{14,18},{18,22},{22,26},{26,30},{7,3},{11,7},... | collective-permute-start | bytes 98312 | tf_op jit(solution)/shard_map/ppermute | solution.py:824
  111.9 5.2 %collective-permute-start.21 = (bf16[144,2048]{1,0:T(8,128)(2,1)S(1)}, bf16[144,2048]{1,0:T(8,128)(2,1)S(1)}, u32[]{:S(2)}, u32[]{:S(2)}) collective-permute-start(bf16[144,2048]{1,0:T(8,128)(2,1)S(1)} %get-tuple-element.120.mine), channel_id=1, source_target_pairs={{2,6},{6,2},{10,14},{14,10},{18,22},{22,18},{26,30},{30,26},{3,7},... | collective-permute-start | bytes 1769480 | tf_op jit(solution)/shard_map/ppermute | solution.py:745
  117.7 12.2 %collective-permute-start.24 = (bf16[144,1024]{1,0:T(8,128)(2,1)S(1)}, bf16[144,1024]{1,0:T(8,128)(2,1)S(1)}, u32[]{:S(2)}, u32[]{:S(2)}) collective-permute-start(bf16[144,1024]{1,0:T(8,128)(2,1)S(1)} %pair.3.refs_0_), channel_id=1, source_target_pairs={{2,26},{6,30},{10,18},{14,22},{19,11},{23,15},{27,3},{31,7}} | collective-permute-start | bytes 884744 | tf_op jit(solution)/shard_map/ppermute | solution.py:754
  119.0 17.1 %collective-permute-start.23 = (bf16[144,1024]{1,0:T(8,128)(2,1)S(1)}, bf16[144,1024]{1,0:T(8,128)(2,1)S(1)}, u32[]{:S(2)}, u32[]{:S(2)}) collective-permute-start(bf16[144,1024]{1,0:T(8,128)(2,1)S(1)} %pair.3.refs_0_), channel_id=1, source_target_pairs={{2,18},{6,22},{10,26},{14,30},{19,3},{23,7},{27,11},{31,15}} | collective-permute-start | bytes 884744 | tf_op jit(solution)/shard_map/ppermute | solution.py:754
  120.3 15.8 %collective-permute-start.22 = (bf16[144,1024]{1,0:T(8,128)(2,1)S(1)}, bf16[144,1024]{1,0:T(8,128)(2,1)S(1)}, u32[]{:S(2)}, u32[]{:S(2)}) collective-permute-start(bf16[144,1024]{1,0:T(8,128)(2,1)S(1)} %pair.3.refs_0_), channel_id=1, source_target_pairs={{2,10},{6,14},{18,26},{22,30},{11,3},{15,7},{27,19},{31,23}} | collective-permute-start | bytes 884744 | tf_op jit(solution)/shard_map/ppermute | solution.py:754
  122.8 17.8 %copy-start.4 = (bf16[128,1024]{1,0:T(8,128)(2,1)S(1)}, bf16[128,1024]{1,0:T(8,128)(2,1)}, u32[]{:S(2)}) copy-start(bf16[128,1024]{1,0:T(8,128)(2,1)} %copy-done.3) | copy-start | bytes 786436
  137.1 3.4 %collective-permute-start.25 = (bf16[128,1024]{1,0:T(8,128)(2,1)S(1)}, bf16[128,1024]{1,0:T(8,128)(2,1)S(1)}, u32[]{:S(2)}, u32[]{:S(2)}) collective-permute-start(bf16[128,1024]{1,0:T(8,128)(2,1)S(1)} %merge.3.refs_6_), channel_id=1, source_target_pairs={{2,6},{6,2},{10,14},{14,10},{18,22},{22,18},{26,30},{30,26},{3,7},... | collective-permute-start | bytes 786440 | tf_op jit(solution)/shard_map/ppermute | solution.py:745
  140.5 9.6 %copy-start.2 = (bf16[128,1024]{1,0:T(8,128)(2,1)S(1)}, bf16[128,1024]{1,0:T(8,128)(2,1)}, u32[]{:S(2)}) copy-start(bf16[128,1024]{1,0:T(8,128)(2,1)} %copy-done.1) | copy-start | bytes 786436
  140.5 9.6 %copy-start.6 = (bf16[128,1024]{1,0:T(8,128)(2,1)S(1)}, bf16[128,1024]{1,0:T(8,128)(2,1)}, u32[]{:S(2)}) copy-start(bf16[128,1024]{1,0:T(8,128)(2,1)} %copy-done.5) | copy-start | bytes 786436
  144.2 18.0 %collective-permute-start.28 = (bf16[128,1024]{1,0:T(8,128)(2,1)S(1)}, bf16[128,1024]{1,0:T(8,128)(2,1)S(1)}, u32[]{:S(2)}, u32[]{:S(2)}) collective-permute-start(bf16[128,1024]{1,0:T(8,128)(2,1)S(1)} %get-tuple-element.140.sent), channel_id=1, source_target_pairs={{2,3},{3,2},{1,0},{6,7},{7,6},{5,4},{10,11},{11,10},{9,8},{14,15},... | collective-permute-start | bytes 786440 | tf_op jit(solution)/shard_map/ppermute | solution.py:938
  146.2 14.7 %collective-permute-start.29 = (bf16[128,1024]{1,0:T(8,128)(2,1)S(1)}, bf16[128,1024]{1,0:T(8,128)(2,1)S(1)}, u32[]{:S(2)}, u32[]{:S(2)}) collective-permute-start(bf16[128,1024]{1,0:T(8,128)(2,1)S(1)} %get-tuple-element.142.sent), channel_id=1, source_target_pairs={{2,3},{3,2},{1,0},{6,7},{7,6},{5,4},{10,11},{11,10},{9,8},{14,15},... | collective-permute-start | bytes 786440 | tf_op jit(solution)/shard_map/ppermute | solution.py:938
  154.6 12.0 %collective-permute-start.27 = (bf16[128,1024]{1,0:T(8,128)(2,1)S(1)}, bf16[128,1024]{1,0:T(8,128)(2,1)S(1)}, u32[]{:S(2)}, u32[]{:S(2)}) collective-permute-start(bf16[128,1024]{1,0:T(8,128)(2,1)S(1)} %get-tuple-element.138.sent), channel_id=1, source_target_pairs={{2,3},{3,2},{1,0},{6,7},{7,6},{5,4},{10,11},{11,10},{9,8},{14,15},... | collective-permute-start | bytes 786440 | tf_op jit(solution)/shard_map/ppermute | solution.py:938
  156.5 14.8 %collective-permute-start.26 = (bf16[128,1024]{1,0:T(8,128)(2,1)S(1)}, bf16[128,1024]{1,0:T(8,128)(2,1)S(1)}, u32[]{:S(2)}, u32[]{:S(2)}) collective-permute-start(bf16[128,1024]{1,0:T(8,128)(2,1)S(1)} %get-tuple-element.136.sent), channel_id=1, source_target_pairs={{2,3},{3,2},{1,0},{6,7},{7,6},{5,4},{10,11},{11,10},{9,8},{14,15},... | collective-permute-start | bytes 786440 | tf_op jit(solution)/shard_map/ppermute | solution.py:938
